TPU v7x, 32 devices: a whole 2x2x4 slice. The times are simulated.
32 devices in a mesh: dp: 8 (over z, core), fsdp: 4 (over y, x).
Axes of the slice: x: 2, y: 2, z: 4, core: 2. Of those that a mesh axis runs over, the one named last changes fastest.
Arguments:
- tokens: bfloat16 [16384, 1024], P(('dp', 'fsdp')), may hold values from -6 to 6
- first_values: bfloat16 [16384, 1024], P(('dp', 'fsdp')), may hold values from -12 to 12
- lengths: int32 [32], P(('dp', 'fsdp')), may hold values from 256 to 512, as said below
- gain_one: bfloat16 [1024], P('fsdp'), may hold values from 0.099609375 to 1.8984375
- w_qkv: bfloat16 [1024, 3072], P('fsdp'), may hold values from -0.1875 to 0.1875
- w_out: bfloat16 [1024, 1024], P('fsdp'), may hold values from -3 to 3
- gain_two: bfloat16 [1024], P('fsdp'), may hold values from 0.099609375 to 1.8984375
- w_gate: bfloat16 [1024, 2816], P('fsdp'), may hold values from -0.1875 to 0.1875
- w_up: bfloat16 [1024, 2816], P('fsdp'), may hold values from -0.1875 to 0.1875
- w_down: bfloat16 [2816, 1024], P('fsdp'), may hold values from -0.4375 to 0.4375
- cotangent: bfloat16 [16384, 1024], P(('dp', 'fsdp')), may hold values from -6 to 6
Outputs:
- output: bfloat16 [16384, 1024], P(('dp', 'fsdp'))
- grad_tokens: float32 [16384, 1024], P(('dp', 'fsdp'))
- grad_first_values: float32 [16384, 1024], P(('dp', 'fsdp'))
- grad_gain_one: float32 [1024], P('fsdp')
- grad_w_qkv: float32 [1024, 3072], P('fsdp')
- grad_w_out: float32 [1024, 1024], P('fsdp')
- grad_gain_two: float32 [1024], P('fsdp')
- grad_w_gate: float32 [1024, 2816], P('fsdp')
- grad_w_up: float32 [1024, 2816], P('fsdp')
- grad_w_down: float32 [2816, 1024], P('fsdp')
- first_norm: float32 [], replicated
- value_norm: float32 [], replicated
Inputs may be any that keep to these rules, and one draw needn't show every extreme that they name: `lengths`: each device holds one whole sequence in its 512 rows; rows from its length on are padding that no query reads.
All inputs are finite; a program needn't handle non-finite values.
Results may differ from a plain program's by a relative error of at most 0.015.
Values may be sent and summed in bfloat16 or wider, within the bound.
A program may use at most 192 MiB of HBM per device.

v0:
```python
import math

import jax
import jax.numpy as jnp
from jax import lax
from jax.sharding import PartitionSpec as P

HEAD_DIM = 64


norm_eps = 1e-06


def rotary_tables(count, width):
    half_width = width // 2
    frequency = jnp.exp(
        -(jnp.arange(half_width, dtype=jnp.float32) * 2.0 / width) * math.log(10000.0)
    )
    angles = jnp.arange(count, dtype=jnp.float32)[:, None] * frequency[None, :]
    cosine = jnp.concatenate([jnp.cos(angles), jnp.cos(angles)], axis=1)
    sine_table = jnp.concatenate([jnp.sin(angles), jnp.sin(angles)], axis=1)
    return (cosine[:, None, :], sine_table[:, None, :])


def rotate(values, cosine, sine_table):
    half_width = values.shape[-1] // 2
    turned = jnp.concatenate([-values[..., half_width:], values[..., :half_width]], axis=-1)
    return values * cosine + turned * sine_table


def unrotate(grads, cosine, sine_table):
    half_width = grads.shape[-1] // 2
    scaled = grads * sine_table
    turned = jnp.concatenate([scaled[..., half_width:], -scaled[..., :half_width]], axis=-1)
    return grads * cosine + turned


def rms_back(grad_normed, normed, inverse):
    return inverse * (grad_normed - normed * jnp.mean(grad_normed * normed, axis=-1, keepdims=True))


def reorder_rows(grad, owners, replicas):
    piece_rows = grad.shape[0] // (owners * replicas)
    shaped = grad.reshape((owners, replicas, piece_rows) + grad.shape[1:])
    return jnp.swapaxes(shaped, 0, 1).reshape(grad.shape)


def body(
    tokens, first_values, lengths, gain_one, w_qkv, w_out, gain_two, w_gate, w_up, w_down, cotangent
):
    gathered = (
        lax.all_gather(gain_one, "fsdp", axis=0, tiled=True),
        lax.all_gather(w_qkv, "fsdp", axis=0, tiled=True),
        lax.all_gather(w_out, "fsdp", axis=0, tiled=True),
        lax.all_gather(gain_two, "fsdp", axis=0, tiled=True),
        lax.all_gather(w_gate, "fsdp", axis=0, tiled=True),
        lax.all_gather(w_up, "fsdp", axis=0, tiled=True),
        lax.all_gather(w_down, "fsdp", axis=0, tiled=True),
    )
    full_gain_one, full_qkv, full_out, full_gain_two, full_gate, full_up, full_down = gathered
    rows, width = tokens.shape
    head_count = width // HEAD_DIM
    block_rows = min(512, rows)
    scale = HEAD_DIM ** (-0.5)
    length = lengths[0]
    inputs = tokens.astype(jnp.float32)
    inverse_one = lax.rsqrt(jnp.mean(inputs * inputs, axis=-1, keepdims=True) + norm_eps)
    normed_one = inputs * inverse_one
    gain_one_f = full_gain_one.astype(jnp.float32)
    hidden_one = (normed_one * gain_one_f).astype(jnp.bfloat16)
    projected = jnp.dot(hidden_one, full_qkv, preferred_element_type=jnp.float32)
    shaped = projected.reshape(rows, 3, head_count, HEAD_DIM)
    cosine, sine_table = rotary_tables(rows, HEAD_DIM)
    queries = rotate(shaped[:, 0], cosine, sine_table).astype(jnp.bfloat16)
    keys_low = rotate(shaped[:, 1], cosine, sine_table).astype(jnp.bfloat16)
    first_float = first_values.astype(jnp.float32).reshape(rows, head_count, HEAD_DIM)
    mixed = 0.5 * shaped[:, 2] + 0.5 * first_float
    values_low = mixed.astype(jnp.bfloat16)
    position = jnp.arange(rows)
    key_live = position < length

    def block_scores(start, query_block):
        scores = (
            jnp.einsum("qhd,khd->hqk", query_block, keys_low, preferred_element_type=jnp.float32)
            * scale
        )
        query_pos = start + jnp.arange(block_rows)
        allowed = (position[None, :] <= query_pos[:, None]) & key_live[None, :]
        return jnp.where(allowed[None], scores, -1e30)

    start = 0
    query_block = queries
    scores = block_scores(start, query_block)
    peak = jnp.max(scores, axis=-1, keepdims=True)
    expo = jnp.exp(scores - peak)
    total = jnp.sum(expo, axis=-1, keepdims=True)
    soft = expo / total
    log_totals = [peak + jnp.log(total)]
    attended_blocks = jnp.einsum(
        "hqk,khd->qhd", soft.astype(jnp.bfloat16), values_low, preferred_element_type=jnp.float32
    )
    attended = attended_blocks.reshape(rows, width).astype(jnp.bfloat16)
    after_attn = inputs + jnp.dot(attended, full_out, preferred_element_type=jnp.float32)
    inverse_two = lax.rsqrt(jnp.mean(after_attn * after_attn, axis=-1, keepdims=True) + norm_eps)
    normed_two = after_attn * inverse_two
    gain_two_f = full_gain_two.astype(jnp.float32)
    hidden_two = (normed_two * gain_two_f).astype(jnp.bfloat16)
    gate_pre = jnp.dot(hidden_two, full_gate, preferred_element_type=jnp.float32)
    up_proj = jnp.dot(hidden_two, full_up, preferred_element_type=jnp.float32)
    sigma = jax.nn.sigmoid(gate_pre)
    activated = gate_pre * sigma
    product = (activated * up_proj).astype(jnp.bfloat16)
    result = (after_attn + jnp.dot(product, full_down, preferred_element_type=jnp.float32)).astype(
        jnp.bfloat16
    )
    norm_sums = lax.psum(
        (jnp.sum(first_float * first_float), jnp.sum(mixed * mixed)), ("dp", "fsdp")
    )
    entry_count = rows * width * lax.axis_size("dp") * lax.axis_size("fsdp")
    first_norm = norm_sums[0] / entry_count
    value_norm = norm_sums[1] / entry_count
    backward_set = (
        lax.all_gather(gain_one, "fsdp", axis=0, tiled=True),
        lax.all_gather(w_qkv, "fsdp", axis=0, tiled=True),
        lax.all_gather(w_out, "fsdp", axis=0, tiled=True),
        lax.all_gather(gain_two, "fsdp", axis=0, tiled=True),
        lax.all_gather(w_gate, "fsdp", axis=0, tiled=True),
        lax.all_gather(w_up, "fsdp", axis=0, tiled=True),
        lax.all_gather(w_down, "fsdp", axis=0, tiled=True),
    )
    qkv_back = backward_set[1]
    out_back = backward_set[2]
    gate_back = backward_set[4]
    up_back = backward_set[5]
    down_back = backward_set[6]
    grad_w_down = jnp.einsum("nf,nd->fd", product, cotangent, preferred_element_type=jnp.float32)
    grad_product = jnp.einsum("nd,fd->nf", cotangent, down_back, preferred_element_type=jnp.float32)
    grad_gate = (grad_product * up_proj * sigma * (1.0 + gate_pre * (1.0 - sigma))).astype(
        jnp.bfloat16
    )
    grad_up = (grad_product * activated).astype(jnp.bfloat16)
    grad_w_gate = jnp.einsum("nd,nf->df", hidden_two, grad_gate, preferred_element_type=jnp.float32)
    grad_w_up = jnp.einsum("nd,nf->df", hidden_two, grad_up, preferred_element_type=jnp.float32)
    grad_hidden_two = jnp.einsum(
        "nf,df->nd", grad_gate, gate_back, preferred_element_type=jnp.float32
    )
    grad_hidden_two = grad_hidden_two + jnp.einsum(
        "nf,df->nd", grad_up, up_back, preferred_element_type=jnp.float32
    )
    grad_gain_two = jnp.sum(grad_hidden_two * normed_two, axis=0)
    grad_after = cotangent.astype(jnp.float32) + rms_back(
        grad_hidden_two * gain_two_f, normed_two, inverse_two
    )
    grad_after_low = grad_after.astype(jnp.bfloat16)
    grad_w_out = jnp.einsum(
        "nd,ne->de", attended, grad_after_low, preferred_element_type=jnp.float32
    )
    grad_attended = jnp.einsum(
        "ne,de->nd", grad_after_low, out_back, preferred_element_type=jnp.float32
    )
    grad_attended = grad_attended.astype(jnp.bfloat16).reshape(rows, head_count, HEAD_DIM)
    grad_keys = jnp.zeros((rows, head_count, HEAD_DIM), jnp.float32)
    grad_values = jnp.zeros((rows, head_count, HEAD_DIM), jnp.float32)
    grad_query_blocks = []
    for block_index, start in enumerate(range(0, rows, block_rows)):
        query_block = queries
        scores = block_scores(start, query_block)
        soft = jnp.exp(scores - log_totals[block_index])
        grad_soft = jnp.einsum(
            "qhd,khd->hqk", grad_attended, values_low, preferred_element_type=jnp.float32
        )
        inner = jnp.sum(soft * grad_soft, axis=-1, keepdims=True)
        grad_scores = (soft * (grad_soft - inner)).astype(jnp.bfloat16)
        grad_query_blocks.append(
            jnp.einsum("hqk,khd->qhd", grad_scores, keys_low, preferred_element_type=jnp.float32)
            * scale
        )
        grad_keys = (
            jnp.einsum("hqk,qhd->khd", grad_scores, query_block, preferred_element_type=jnp.float32)
            * scale
        )
        grad_values = jnp.einsum(
            "hqk,qhd->khd",
            soft.astype(jnp.bfloat16),
            grad_attended,
            preferred_element_type=jnp.float32,
        )
    grad_queries = grad_query_blocks[0]
    grad_first = (0.5 * grad_values).reshape(rows, width)
    grad_projected = jnp.stack(
        [
            unrotate(grad_queries, cosine, sine_table),
            unrotate(grad_keys, cosine, sine_table),
            0.5 * grad_values,
        ],
        axis=1,
    )
    grad_projected = grad_projected.reshape(rows, 3 * width).astype(jnp.bfloat16)
    grad_w_qkv = jnp.einsum(
        "nd,ne->de", hidden_one, grad_projected, preferred_element_type=jnp.float32
    )
    grad_hidden_one = jnp.einsum(
        "ne,de->nd", grad_projected, qkv_back, preferred_element_type=jnp.float32
    )
    grad_gain_one = jnp.sum(grad_hidden_one * normed_one, axis=0)
    grad_tokens = grad_after + rms_back(grad_hidden_one * gain_one_f, normed_one, inverse_one)
    owners = lax.axis_size("fsdp")
    replicas = lax.axis_size("dp")
    pieces = (
        lax.psum_scatter(
            reorder_rows(grad_gain_one, owners, replicas),
            ("dp", "fsdp"),
            scatter_dimension=0,
            tiled=True,
        ),
        lax.psum_scatter(
            reorder_rows(grad_w_qkv, owners, replicas),
            ("dp", "fsdp"),
            scatter_dimension=0,
            tiled=True,
        ),
        lax.psum_scatter(
            reorder_rows(grad_w_out, owners, replicas),
            ("dp", "fsdp"),
            scatter_dimension=0,
            tiled=True,
        ),
        lax.psum_scatter(
            reorder_rows(grad_gain_two, owners, replicas),
            ("dp", "fsdp"),
            scatter_dimension=0,
            tiled=True,
        ),
        lax.psum_scatter(
            reorder_rows(grad_w_gate, owners, replicas),
            ("dp", "fsdp"),
            scatter_dimension=0,
            tiled=True,
        ),
        lax.psum_scatter(
            reorder_rows(grad_w_up, owners, replicas),
            ("dp", "fsdp"),
            scatter_dimension=0,
            tiled=True,
        ),
        lax.psum_scatter(
            reorder_rows(grad_w_down, owners, replicas),
            ("dp", "fsdp"),
            scatter_dimension=0,
            tiled=True,
        ),
    )
    shards = (
        lax.all_gather(pieces[0].astype(jnp.bfloat16), "dp", axis=0, tiled=True).astype(
            jnp.float32
        ),
        lax.all_gather(pieces[1].astype(jnp.bfloat16), "dp", axis=0, tiled=True).astype(
            jnp.float32
        ),
        lax.all_gather(pieces[2].astype(jnp.bfloat16), "dp", axis=0, tiled=True).astype(
            jnp.float32
        ),
        lax.all_gather(pieces[3].astype(jnp.bfloat16), "dp", axis=0, tiled=True).astype(
            jnp.float32
        ),
        lax.all_gather(pieces[4].astype(jnp.bfloat16), "dp", axis=0, tiled=True).astype(
            jnp.float32
        ),
        lax.all_gather(pieces[5].astype(jnp.bfloat16), "dp", axis=0, tiled=True).astype(
            jnp.float32
        ),
        lax.all_gather(pieces[6].astype(jnp.bfloat16), "dp", axis=0, tiled=True).astype(
            jnp.float32
        ),
    )
    return (
        result,
        grad_tokens,
        grad_first,
        shards[0],
        shards[1],
        shards[2],
        shards[3],
        shards[4],
        shards[5],
        shards[6],
        first_norm,
        value_norm,
    )


def solution(mesh):
    in_specs = (
        P(("dp", "fsdp"), None),
        P(("dp", "fsdp"), None),
        P(("dp", "fsdp")),
        P("fsdp"),
        P("fsdp", None),
        P("fsdp", None),
        P("fsdp"),
        P("fsdp", None),
        P("fsdp", None),
        P("fsdp", None),
        P(("dp", "fsdp"), None),
    )
    out_specs = (
        P(("dp", "fsdp"), None),
        P(("dp", "fsdp"), None),
        P(("dp", "fsdp"), None),
        P("fsdp"),
        P("fsdp", None),
        P("fsdp", None),
        P("fsdp"),
        P("fsdp", None),
        P("fsdp", None),
        P("fsdp", None),
        P(),
        P(),
    )
    return jax.shard_map(body, mesh=mesh, in_specs=in_specs, out_specs=out_specs, check_vma=False)
```

profile of v0, /device:TPU:0, one launch (start us, length us, event | category | flops | bytes accessed | tf_op | source)
XLA Modules:
  0.0 1591.4 jit_solution(17329007705025905702)
XLA Ops:
  32.9 49.9 %all-gather.12.cloned.1.call-done = bf16[1024,3072]{1,0:T(8,128)(2,1)} async-done(((bf16[256,3072]{1,0:T(8,128)(2,1)}), bf16[1024,3072]{1,0:T(8,128)(2,1)}) %all-gather.12.cloned.1.call-update) | async-done | bytes 6291472 | tf_op jit(solution)/shard_map/all_gather | solution.py:53
  124.7 62.9 %all-gather.18.cloned.1.call-done = bf16[1024,2816]{1,0:T(8,128)(2,1)} async-done(((bf16[256,2816]{1,0:T(8,128)(2,1)}), bf16[1024,2816]{1,0:T(8,128)(2,1)}) %all-gather.18.cloned.1.call-update) | async-done | bytes 5767184 | tf_op jit(solution)/shard_map/all_gather | solution.py:57
  196.2 59.0 %all-gather.16.cloned.1.call-done = bf16[1024,2816]{1,0:T(8,128)(2,1)} async-done(((bf16[256,2816]{1,0:T(8,128)(2,1)}), bf16[1024,2816]{1,0:T(8,128)(2,1)}) %all-gather.16.cloned.1.call-update) | async-done | bytes 5767184 | tf_op jit(solution)/shard_map/all_gather | solution.py:56
  263.7 59.0 %all-gather.20.cloned.1.call-done = bf16[2816,1024]{1,0:T(8,128)(2,1)} async-done(((bf16[704,1024]{1,0:T(8,128)(2,1)}), bf16[2816,1024]{1,0:T(8,128)(2,1)}) %all-gather.20.cloned.1.call-update) | async-done | bytes 5767184 | tf_op jit(solution)/shard_map/all_gather | solution.py:58
  322.7 11.3 multiply_convert_fusion.1
  348.1 9.9 fusion.26
  358.0 14.6 multiply_reduce_fusion
  399.3 10.2 convolution_bitcast_fusion
  409.5 10.7 copy.81
  430.1 11.9 copy.86
  442.1 10.1 fusion.49
  452.2 10.7 copy.85
  473.0 10.8 copy.84
  489.3 86.5 %reduce-scatter.6.cloned.1.call-done = f32[32,3072]{1,0:T(8,128)} async-done(((f32[1024,3072]{1,0:T(8,128)}), f32[32,3072]{1,0:T(8,128)}) %reduce-scatter.6.cloned.1.call-update) | async-done | bytes 393232 | tf_op jit(solution)/shard_map/reduce_scatter | solution.py:216
  577.6 248.5 %reduce-scatter.14.cloned.1.call-done = f32[88,1024]{1,0:T(8,128)} async-done(((f32[2816,1024]{1,0:T(8,128)}), f32[88,1024]{1,0:T(8,128)}) %reduce-scatter.14.cloned.1.call-update) | async-done | bytes 360464 | tf_op jit(solution)/shard_map/reduce_scatter | solution.py:246
  827.9 250.6 %reduce-scatter.12.cloned.1.call-done = f32[32,2816]{1,0:T(8,128)} async-done(((f32[1024,2816]{1,0:T(8,128)}), f32[32,2816]{1,0:T(8,128)}) %reduce-scatter.12.cloned.1.call-update) | async-done | bytes 360464 | tf_op jit(solution)/shard_map/reduce_scatter | solution.py:240
  1080.2 250.6 %reduce-scatter.10.cloned.1.call-done = f32[32,2816]{1,0:T(8,128)} async-done(((f32[1024,2816]{1,0:T(8,128)}), f32[32,2816]{1,0:T(8,128)}) %reduce-scatter.10.cloned.1.call-update) | async-done | bytes 360464 | tf_op jit(solution)/shard_map/reduce_scatter | solution.py:234
  1338.3 42.0 %all-reduce.4 = (bf16[1024]{0:T(1024)(128)(2,1)S(1)}, bf16[1024]{0:T(1024)(128)(2,1)S(1)}, f32[]{:T(128)}, f32[]{:T(128)}) all-reduce(f32[1024]{0:T(1024)S(1)} %reshape.169, f32[1024]{0:T(1024)S(1)} %reshape.173, f32[]{:T(128)} %multiply_reduce_fusion.2, f32[]{:T(128)} %get-tuple-element.77), channel_id=2, replica_groups=mesh['dp'=8,'fsdp'=4] {'dp','fsdp'}, use_global_device_ids=true, to_apply=%region_8.9.clone | all-reduce | flops 2050 | bytes 12304
  1382.2 15.8 all-reduce.5
  1410.2 66.0 %reduce-scatter.8.cloned.1.call-done = f32[32,1024]{1,0:T(8,128)} async-done(((f32[1024,1024]{1,0:T(8,128)}), f32[32,1024]{1,0:T(8,128)}) %reduce-scatter.8.cloned.1.call-update) | async-done | bytes 131088 | tf_op jit(solution)/shard_map/reduce_scatter | solution.py:222
  1477.1 16.1 %all_gather.56 = bf16[256,1024]{1,0:T(8,128)(2,1)S(1)} all-gather(bf16[32,1024]{1,0:T(8,128)(2,1)S(1)} %convert_element_type.149), channel_id=1, replica_groups=mesh['dp'=8,'fsdp'=4] {'dp'}, dimensions={0}, use_global_device_ids=true | all-gather | bytes 589824 | tf_op jit(solution)/shard_map/all_gather | solution.py:260
  1506.0 21.4 %all-gather.28.cloned.1.call-done = bf16[704,1024]{1,0:T(8,128)(2,1)} async-done(((bf16[88,1024]{1,0:T(8,128)(2,1)}), bf16[704,1024]{1,0:T(8,128)(2,1)}) %all-gather.28.cloned.1.call-update) | async-done | bytes 1441808 | tf_op jit(solution)/shard_map/all_gather | solution.py:272
  1530.7 22.3 %all-gather.26.cloned.1.call-done = bf16[256,2816]{1,0:T(8,128)(2,1)} async-done(((bf16[32,2816]{1,0:T(8,128)(2,1)}), bf16[256,2816]{1,0:T(8,128)(2,1)}) %all-gather.26.cloned.1.call-update) | async-done | bytes 1441808 | tf_op jit(solution)/shard_map/all_gather | solution.py:269
  1556.1 22.9 %all-gather.24.cloned.1.call-done = bf16[256,2816]{1,0:T(8,128)(2,1)} async-done(((bf16[32,2816]{1,0:T(8,128)(2,1)}), bf16[256,2816]{1,0:T(8,128)(2,1)}) %all-gather.24.cloned.1.call-update) | async-done | bytes 1441808 | tf_op jit(solution)/shard_map/all_gather | solution.py:266
  (176 shorter events, 197.8 us)
Async XLA Ops:
  7.2 75.6 %all-gather.12.cloned.1.call-start = ((), (), s32[]{:S(2)}) async-start(), calls=%async_computation.5 | async-start | bytes 7864320 | tf_op jit(solution)/shard_map/all_gather | solution.py:53
  7.9 112.0 %all-gather.14.cloned.1.call-start = ((), (), s32[]{:S(2)}) async-start(), calls=%async_computation.6 | async-start | bytes 2621440 | tf_op jit(solution)/shard_map/all_gather | solution.py:54
  8.7 21.7 %copy-start.14 = (bf16[512,1024]{1,0:T(8,128)(2,1)S(1)}, bf16[512,1024]{1,0:T(8,128)(2,1)}, u32[]{:S(2)}) copy-start(bf16[512,1024]{1,0:T(8,128)(2,1)} %param.12) | copy-start | bytes 3145732
  8.7 179.0 %all-gather.18.cloned.1.call-start = ((), (), s32[]{:S(2)}) async-start(), calls=%async_computation.8 | async-start | bytes 7208960 | tf_op jit(solution)/shard_map/all_gather | solution.py:57
  9.4 245.8 %all-gather.16.cloned.1.call-start = ((), (), s32[]{:S(2)}) async-start(), calls=%async_computation.7 | async-start | bytes 7208960 | tf_op jit(solution)/shard_map/all_gather | solution.py:56
  10.0 312.7 %all-gather.20.cloned.1.call-start = ((), (), s32[]{:S(2)}) async-start(), calls=%async_computation.9 | async-start | bytes 7208960 | tf_op jit(solution)/shard_map/all_gather | solution.py:58
  10.6 565.2 %reduce-scatter.6.cloned.1.call-start = ((), (), s32[]{:S(2)}) async-start(), calls=%async_computation.10 | async-start | bytes 12976128 | tf_op jit(solution)/shard_map/reduce_scatter | solution.py:216
  30.9 57.7 %copy-start.8 = (bf16[512,1024]{0,1:T(8,128)(2,1)}, bf16[512,1024]{0,1:T(8,128)(2,1)S(1)}, u32[]{:S(2)}) copy-start(bf16[512,1024]{0,1:T(8,128)(2,1)S(1)} %copy.72) | copy-start | bytes 3145732
  89.2 19.7 %copy-start.11 = (bf16[512,16,64]{0,2,1:T(8,128)(2,1)}, bf16[512,16,64]{0,2,1:T(8,128)(2,1)S(1)}, u32[]{:S(2)}) copy-start(bf16[512,16,64]{0,2,1:T(8,128)(2,1)S(1)} %get-tuple-element.70) | copy-start | bytes 3145732
  123.3 220.1 %copy-start.1 = (f32[512,1024]{1,0:T(8,128)}, f32[512,1024]{1,0:T(8,128)S(1)}, u32[]{:S(2)}) copy-start(f32[512,1024]{1,0:T(8,128)S(1)} %get-tuple-element.102) | copy-start | bytes 6291460
  123.3 223.8 %copy-start.19 = (f32[16,512]{1,0:T(8,128)}, f32[16,512]{1,0:T(8,128)S(1)}, u32[]{:S(2)}) copy-start(f32[16,512]{1,0:T(8,128)S(1)} %log_add_fusion) | copy-start | bytes 98308
  348.1 24.5 %slice-start = ((s8[16777216]{0:T(1024)(128)(4,1)}), s8[4194304]{0:T(1024)(128)(4,1)S(1)}, s32[]{:S(2)}) async-start(s8[16777216]{0:T(1024)(128)(4,1)} %bitcast.121), calls=%async_computation.19 | async-start | bytes 8388608
  348.1 24.5 %slice-start.1 = ((s8[16777216]{0:T(1024)(128)(4,1)}), s8[4194304]{0:T(1024)(128)(4,1)S(1)}, s32[]{:S(2)}) async-start(s8[16777216]{0:T(1024)(128)(4,1)} %bitcast.121), calls=%async_computation.20 | async-start | bytes 8388608
  358.0 14.6 slice-start.2
  358.0 14.6 slice-start.3
  420.3 405.8 %reduce-scatter.14.cloned.1.call-start = ((), (), s32[]{:S(2)}) async-start(), calls=%async_computation.17 | async-start | bytes 11894784 | tf_op jit(solution)/shard_map/reduce_scatter | solution.py:246
  442.0 636.4 %reduce-scatter.12.cloned.1.call-start = ((), (), s32[]{:S(2)}) async-start(), calls=%async_computation.15 | async-start | bytes 11894784 | tf_op jit(solution)/shard_map/reduce_scatter | solution.py:240
  462.9 867.9 %reduce-scatter.10.cloned.1.call-start = ((), (), s32[]{:S(2)}) async-start(), calls=%async_computation.13 | async-start | bytes 11894784 | tf_op jit(solution)/shard_map/reduce_scatter | solution.py:234
  483.8 992.4 %reduce-scatter.8.cloned.1.call-start = ((), (), s32[]{:S(2)}) async-start(), calls=%async_computation.12 | async-start | bytes 4325376 | tf_op jit(solution)/shard_map/reduce_scatter | solution.py:222
  489.3 843.3 %copy-start.23 = (u32[32]{0:T(128)S(1)}, u32[32]{0:T(128)}, u32[]{:S(2)}) copy-start(u32[32]{0:T(128)} %constant.35) | copy-start | bytes 388
  489.3 1013.3 %all-gather.22.cloned.1.call-start = ((), (), s32[]{:S(2)}) async-start(), calls=%async_computation.11 | async-start | bytes 1769472 | tf_op jit(solution)/shard_map/all_gather | solution.py:257
  577.5 949.8 %all-gather.28.cloned.1.call-start = ((), (), s32[]{:S(2)}) async-start(), calls=%async_computation.18 | async-start | bytes 1622016 | tf_op jit(solution)/shard_map/all_gather | solution.py:272
  827.8 725.2 %all-gather.26.cloned.1.call-start = ((), (), s32[]{:S(2)}) async-start(), calls=%async_computation.16 | async-start | bytes 1622016 | tf_op jit(solution)/shard_map/all_gather | solution.py:269
  1080.2 498.9 %all-gather.24.cloned.1.call-start = ((), (), s32[]{:S(2)}) async-start(), calls=%async_computation.14 | async-start | bytes 1622016 | tf_op jit(solution)/shard_map/all_gather | solution.py:266
  (23 other events, 86.7 us)
Sparse Core Ops, SparseCore 0:
  9.9 72.8 all-gather.11
  84.6 35.3 all-gather.13
  121.8 65.7 all-gather.17
  189.4 65.7 all-gather.15
  256.9 65.7 all-gather.19
  420.4 155.3 reduce-scatter.5
  578.3 247.8 reduce-scatter.13
  828.5 249.8 reduce-scatter.11
  1080.9 249.8 reduce-scatter.9
  1333.1 143.0 reduce-scatter.7
  1478.5 24.0 all-gather.21
  1504.2 23.1 all-gather.27
  1529.1 23.8 all-gather.25
  1555.2 23.8 all-gather.23
where the time goes:
time: 1600 us; the launch traced here: 1590 us
  waiting for transfers between devices  1210 us (76%)
  matrix products  147 us (9%)
  blocking collectives  91.5 us (6%)
  local copies, waits for them, and re-layouts  59.5 us (4%)
  other arithmetic  58.7 us (4%)
  between operations  19.8 us (1%)
    reduce_scatter x1, waiting for transfers between devices, body(): lax.psum_scatter(reorder_rows(grad_w_gate, owners, replicas), ('dp', 'fsd...  251 us
    reduce_scatter x1, waiting for transfers between devices, body(): lax.psum_scatter(reorder_rows(grad_w_up, owners, replicas), ('dp', 'fsdp'...  251 us
    reduce_scatter x1, waiting for transfers between devices, body(): lax.psum_scatter(reorder_rows(grad_w_down, owners, replicas), ('dp', 'fsd...  249 us
    reduce_scatter x1, waiting for transfers between devices, body(): lax.psum_scatter(reorder_rows(grad_w_qkv, owners, replicas), ('dp', 'fsdp...  86.5 us
    reduce_scatter x1, waiting for transfers between devices, body(): lax.psum_scatter(reorder_rows(grad_w_out, owners, replicas), ('dp', 'fsdp...  66 us
    all_gather x1, waiting for transfers between devices, body(): lax.all_gather(w_up, 'fsdp', axis=0, tiled=True)  62.9 us
    all_gather x1, waiting for transfers between devices, body(): lax.all_gather(w_down, 'fsdp', axis=0, tiled=True)  59 us
    all_gather x1, waiting for transfers between devices, body(): lax.all_gather(w_gate, 'fsdp', axis=0, tiled=True)  59 us
  transfers between devices with their start and end apart: 14, of which 14 were waited for; matrix products, arithmetic and copies ran while one was open for 10% of the time, Pallas kernels for 0%

commit v1 on v0

v1 whole, which is shorter than its diff:
```python
import functools
import math

import jax
import jax.numpy as jnp
import numpy as np
from jax import lax
from jax.experimental import pallas as pl
from jax.experimental.pallas import tpu as pltpu
from jax.sharding import PartitionSpec as P

HEAD_DIM = 64
PAIR = 2 * HEAD_DIM
TILE = 256
GAIN_ROWS = 16
norm_eps = 1e-06
F32 = jnp.float32
BF16 = jnp.bfloat16
AXES = ("dp", "fsdp")
ANY = pl.BlockSpec(memory_space=pl.ANY)


def dot_nn(a, b):
    return lax.dot_general(a, b, (((1,), (0,)), ((), ())), preferred_element_type=F32)


def dot_nt(a, b):
    return lax.dot_general(a, b, (((1,), (1,)), ((), ())), preferred_element_type=F32)


def rotary_tables(count):
    half = HEAD_DIM // 2
    frequency = np.exp(
        -(np.arange(half, dtype=np.float32) * np.float32(2.0) / np.float32(HEAD_DIM))
        * np.float32(math.log(10000.0))
    ).astype(np.float32)
    angles = np.arange(count, dtype=np.float32)[:, None] * frequency[None, :]
    cosine = np.cos(angles.astype(np.float64)).astype(np.float32)
    sine = np.sin(angles.astype(np.float64)).astype(np.float32)
    cosine = np.concatenate([cosine] * 4, axis=1)
    sine = np.concatenate([-sine, sine, -sine, sine], axis=1)
    return cosine, sine


def swap_halves(x):
    half = HEAD_DIM // 2
    lane = lax.broadcasted_iota(jnp.int32, x.shape, 1)
    up = pltpu.roll(x, PAIR - half, 1)
    down = pltpu.roll(x, half, 1)
    return jnp.where((lane % HEAD_DIM) < half, up, down)


def bit_reverse(value, bits):
    out = 0
    for i in range(bits):
        out = out + ((value >> i) & 1) * (1 << (bits - 1 - i))
    return out


class Layout:
    def __init__(self, dp, fs):
        self.dp, self.fs = dp, fs
        self.bits = fs.bit_length() - 1
        self.line = dp // 2

    def perm(self, move):
        pairs = []
        for d in range(self.dp):
            for f in range(self.fs):
                target = move(d, f)
                if target is not None:
                    pairs.append((d * self.fs + f, target[0] * self.fs + target[1]))
        return pairs

    def send(self, x, move):
        return lax.ppermute(x, AXES, self.perm(move))

    def core(self, x):
        return self.send(x, lambda d, f: (d ^ 1, f))

    def step(self, x, i):
        bits = self.bits
        return self.send(x, lambda d, f: (d, f ^ (1 << (i if d % 2 == 0 else bits - 1 - i))))

    def index(self, length):
        d, f = lax.axis_index("dp"), lax.axis_index("fsdp")
        c = d % 2
        masks = jnp.arange(self.fs, dtype=jnp.int32)
        turned = bit_reverse(masks, self.bits)
        straight = c == 0
        mine = f ^ jnp.where(straight, masks, turned)
        other = f ^ jnp.where(straight, turned, masks)
        order = f ^ jnp.where(straight, turned, masks)
        head = jnp.stack([c, 1 - c, length, f]).astype(jnp.int32)
        return jnp.concatenate([head, mine, other, order]).astype(jnp.int32)

    def gather(self, half):
        pieces = [half]
        for i in range(self.bits):
            pieces = pieces + [self.step(piece, i) for piece in pieces]
        return pieces, [self.core(piece) for piece in pieces[1:]]

    def line_sum(self, total):
        size = self.line
        if size == 1:
            return total
        half = size // 2
        r = lax.axis_index("dp") // 2

        def hop(x, table):
            return self.send(
                x, lambda d, f: (table[d // 2] * 2 + d % 2, f) if d // 2 in table else None
            )

        for i in range(half - 1):
            got = hop(total, {i: i + 1, size - 1 - i: size - 2 - i})
            total = add_low(total, got)
        got = hop(total, {half - 1: half, half: half - 1})
        total = add_low(total, got)
        for i in range(half - 1):
            low, high = half - 1 - i, half + i
            got = hop(total, {low: low - 1, high: high + 1})
            total = jnp.where((r == low - 1) | (r == high + 1), got, total)
        return total

    def reduce(self, keep, send):
        for i in range(self.bits):
            got = self.step(send, i)
            total = add_low(keep, got)
            blocks = total.shape[0]
            if blocks > 1:
                keep, send = total[: blocks // 2], total[blocks // 2 :]
        return self.line_sum(total[0])

    def small_sum(self, x):
        x = x + self.core(x)
        for i in range(self.bits):
            x = x + self.step(x, i)
        reach = 1
        while reach < self.line:
            x = x + self.send(x, lambda d, f: ((((d // 2) ^ reach) * 2 + d % 2), f))
            reach *= 2
        return x


def add_low(a, b):
    return (a.astype(F32) + b.astype(F32)).astype(BF16)


IDX_HEAD = 4


def piece_copies(idx, own, mine, other, target, sems, first, column, width, rows, count):
    copies = [
        pltpu.make_async_copy(own, target.at[pl.ds(idx[3] * rows, rows), :], sems.at[first])
    ]
    for m in range(1, count):
        for which, (pieces, base) in enumerate(((mine, 0), (other, count))):
            shard = idx[IDX_HEAD + base + m]
            side = pl.multiple_of(idx[which] * width, 128)
            copies.append(
                pltpu.make_async_copy(
                    pieces[m - 1].at[pl.ds(0, rows), pl.ds(column, width)],
                    target.at[pl.ds(shard * rows, rows), pl.ds(side, width)],
                    sems.at[first + 2 * m - 1 + which],
                )
            )
    return copies


def start(copies):
    for copy in copies:
        copy.start()


def wait(copies):
    for copy in copies:
        copy.wait()


def call(body, grid, in_specs, out_specs, out_shape, scratch, name, flops, nbytes, limit=56):
    return pl.pallas_call(
        body,
        grid_spec=pltpu.PrefetchScalarGridSpec(
            num_scalar_prefetch=1,
            grid=grid,
            in_specs=in_specs,
            out_specs=out_specs,
            scratch_shapes=scratch,
        ),
        out_shape=out_shape,
        compiler_params=pltpu.CompilerParams(vmem_limit_bytes=limit * 2**20),
        cost_estimate=pl.CostEstimate(
            flops=int(flops), bytes_accessed=int(nbytes), transcendentals=0
        ),
        name=name,
    )


def whole(shape):
    zeros = (0,) * len(shape)
    return pl.BlockSpec(shape, lambda *_: zeros)


def struct(shape, dtype):
    return jax.ShapeDtypeStruct(shape, dtype)


def qkv_body(count, idx, tokens, first, cosine, sine, own, *rest):
    pieces, rest = rest[: 2 * count - 1], rest[2 * count - 1 :]
    queries, keys, values, hidden_t, gains, sums, weight, hidden, gain, sems = rest
    half_own, mine, other = pieces[0], pieces[1:count], pieces[count:]
    rows = own.shape[0]
    width = tokens.shape[1]
    side = own.shape[1] // 2
    copies = piece_copies(idx, own, mine, other, weight, sems, 0, 0, side, rows, count)
    start(copies)
    gain_copies = []
    for m in range(count):
        piece = half_own if m == 0 else mine[m - 1]
        shard = idx[IDX_HEAD + m]
        for which in range(2):
            gain_copies.append(
                pltpu.make_async_copy(
                    piece.at[pl.ds(rows, GAIN_ROWS), pl.ds(which * rows, rows)],
                    gain.at[which, :, pl.ds(pl.multiple_of(shard * rows, 128), rows)],
                    sems.at[2 * count - 1 + 2 * m + which],
                )
            )
    start(gain_copies)
    inputs = tokens[...].astype(F32)
    inverse = lax.rsqrt(jnp.mean(inputs * inputs, axis=-1, keepdims=True) + norm_eps)
    wait(gain_copies)
    gain_one = gain[0, 0:1, :].astype(F32)
    gains[0:1, :] = gain_one
    gains[1:2, :] = gain[1, 0:1, :].astype(F32)
    gains[2:8, :] = jnp.zeros((6, width), F32)
    normed = inputs * inverse * gain_one
    hidden[...] = normed.astype(BF16)
    hidden_t[...] = normed.astype(BF16).T
    wait(copies)
    cos, sin = cosine[...], sine[...]

    def rotated(base, out, scale):
        @pl.loop(0, width // TILE)
        def _(t):
            at = pl.multiple_of(t * TILE, TILE)
            raw = dot_nn(hidden[...], weight[:, pl.ds(base + at, TILE)])
            for part in range(TILE // PAIR):
                x = raw[:, part * PAIR : (part + 1) * PAIR]
                turned = x * cos + swap_halves(x) * sin
                out[:, pl.ds(at + part * PAIR, PAIR)] = turned.astype(BF16) * scale

    rotated(0, queries, jnp.asarray(HEAD_DIM**-0.5, BF16))
    rotated(width, keys, jnp.asarray(1.0, BF16))

    def mix(t, carry):
        at = pl.multiple_of(t * TILE, TILE)
        raw = dot_nn(hidden[...], weight[:, pl.ds(2 * width + at, TILE)])
        kept = first[:, pl.ds(at, TILE)].astype(F32)
        mixed = 0.5 * raw + 0.5 * kept
        values[:, pl.ds(at, TILE)] = mixed.astype(BF16)
        return (
            carry[0] + jnp.sum(kept * kept, axis=0, keepdims=True),
            carry[1] + jnp.sum(mixed * mixed, axis=0, keepdims=True),
        )

    zero = jnp.zeros((1, TILE), F32)
    one, two = lax.fori_loop(0, width // TILE, mix, (zero, zero))
    sums[...] = jnp.zeros(sums.shape, F32)
    sums[0:1, :] = one
    sums[1:2, :] = two


def qkv_kernel(lay, idx, tokens, first, tables, own, half_own, mine, other):
    count = lay.fs
    rows, width = tokens.shape
    n = own.shape[1]
    operands = (tokens, first, tables[0], tables[1], own, half_own, *mine, *other)
    return call(
        functools.partial(qkv_body, count),
        (1,),
        [whole(tokens.shape), whole(first.shape), whole(tables[0].shape), whole(tables[1].shape)]
        + [ANY] * (2 * count),
        [
            whole((rows, width)),
            whole((rows, width)),
            whole((rows, width)),
            whole((width, rows)),
            whole((8, width)),
            whole((8, TILE)),
        ],
        [
            struct((rows, width), BF16),
            struct((rows, width), BF16),
            struct((rows, width), BF16),
            struct((width, rows), BF16),
            struct((8, width), F32),
            struct((8, TILE), F32),
        ],
        [
            pltpu.VMEM((width, n), BF16),
            pltpu.VMEM((rows, width), BF16),
            pltpu.VMEM((2, GAIN_ROWS, width), BF16),
            pltpu.SemaphoreType.DMA((4 * count - 1,)),
        ],
        "qkv",
        2 * rows * width * n,
        2 * width * n + 12 * rows * width,
    )(idx, *operands)


def attend_body(idx, queries, keys, values, attended, attended_t, logs, turned):
    rows = queries.shape[0]
    block = min(TILE, rows)
    length = idx[2]
    lane = lax.broadcasted_iota(jnp.int32, (rows, PAIR), 1)
    q, k = queries[...], keys[...]
    v_t = values[...].T
    logs[...] = jnp.zeros(logs.shape, F32)
    for head in range(2):
        inside = (lane // HEAD_DIM) == head
        k_head = jnp.where(inside, k, jnp.zeros_like(k))
        v_head = v_t[head * HEAD_DIM : (head + 1) * HEAD_DIM]
        for b in range(rows // block):
            upto = (b + 1) * block
            scores = dot_nt(k_head[:upto], q[b * block : upto])
            key = lax.broadcasted_iota(jnp.int32, scores.shape, 0)
            query = lax.broadcasted_iota(jnp.int32, (1, block), 1) + b * block
            scores = jnp.where(key <= jnp.minimum(query, length - 1), scores, -1e30)
            peak = jnp.max(scores, axis=0, keepdims=True)
            expo = jnp.exp(scores - peak)
            total = jnp.sum(expo, axis=0, keepdims=True)
            soft = (expo * (1.0 / total)).astype(BF16)
            logs[0, head : head + 1, b * block : upto] = peak + jnp.log(total)
            turned[head * HEAD_DIM : (head + 1) * HEAD_DIM, b * block : upto] = dot_nn(
                v_head[:, :upto], soft
            )
    out = turned[...]
    attended_t[...] = out.astype(BF16)
    attended[...] = out.T.astype(BF16)


def attend_kernel(idx, queries, keys, values):
    rows, width = queries.shape
    pairs = width // PAIR
    column = pl.BlockSpec((rows, PAIR), lambda p, _: (0, p))
    return call(
        attend_body,
        (pairs,),
        [column] * 3,
        [
            column,
            pl.BlockSpec((PAIR, rows), lambda p, _: (p, 0)),
            pl.BlockSpec((1, 8, rows), lambda p, _: (p, 0, 0)),
        ],
        [
            struct((rows, width), BF16),
            struct((width, rows), BF16),
            struct((pairs, 8, rows), F32),
        ],
        [pltpu.VMEM((PAIR, rows), F32)],
        "attend",
        8 * rows * rows * width,
        10 * rows * width,
        32,
    )(idx, queries, keys, values)


def attend_back_body(
    idx, queries, keys, values, grads, logs, cosine, sine, grad_q, grad_k, grad_v, grad_first, turned
):
    rows = queries.shape[0]
    block = min(TILE, rows)
    length = idx[2]
    lane = lax.broadcasted_iota(jnp.int32, (rows, PAIR), 1)
    q, k, v, g = queries[...], keys[...], values[...], grads[...]
    k_t = k.T
    sums_k, sums_v = [], []
    for head in range(2):
        inside = (lane // HEAD_DIM) == head
        k_head = jnp.where(inside, k, jnp.zeros_like(k))
        v_head = jnp.where(inside, v, jnp.zeros_like(v))
        k_turned = k_t[head * HEAD_DIM : (head + 1) * HEAD_DIM]
        parts_k, parts_v = [], []
        for b in range(rows // block):
            upto = (b + 1) * block
            q_block, g_block = q[b * block : upto], g[b * block : upto]
            scores = dot_nt(k_head[:upto], q_block)
            key = lax.broadcasted_iota(jnp.int32, scores.shape, 0)
            query = lax.broadcasted_iota(jnp.int32, (1, block), 1) + b * block
            log_total = logs[0, head : head + 1, b * block : upto]
            soft = jnp.where(
                key <= jnp.minimum(query, length - 1), jnp.exp(scores - log_total), 0.0
            )
            grad_soft = dot_nt(v_head[:upto], g_block)
            inner = jnp.sum(soft * grad_soft, axis=0, keepdims=True)
            grad_scores = (soft * (grad_soft - inner)).astype(BF16)
            turned[head * HEAD_DIM : (head + 1) * HEAD_DIM, b * block : upto] = dot_nn(
                k_turned[:, :upto], grad_scores
            )
            parts_k.append(dot_nn(grad_scores, q_block))
            parts_v.append(dot_nn(soft.astype(BF16), g_block))
        for parts, sums in ((parts_k, sums_k), (parts_v, sums_v)):
            rows_of = []
            for r in range(rows // block):
                piece = parts[r][r * block : (r + 1) * block]
                for later in parts[r + 1 :]:
                    piece = piece + later[r * block : (r + 1) * block]
                rows_of.append(piece)
            sums.append(jnp.concatenate(rows_of, axis=0))
    first_head = lane < HEAD_DIM
    cos, sin = cosine[...], sine[...]

    def back(x):
        return (x * cos - swap_halves(x) * sin).astype(BF16)

    grad_q[...] = back(turned[...].T * HEAD_DIM**-0.5)
    grad_k[...] = back(jnp.where(first_head, sums_k[0], sums_k[1]))
    half_v = 0.5 * jnp.where(first_head, sums_v[0], sums_v[1])
    grad_first[...] = half_v
    grad_v[...] = half_v.astype(BF16)


def attend_back_kernel(idx, queries, keys, values, grads, logs, tables):
    rows, width = queries.shape
    pairs = width // PAIR
    column = pl.BlockSpec((rows, PAIR), lambda p, _: (0, p))
    return call(
        attend_back_body,
        (pairs,),
        [column] * 4
        + [
            pl.BlockSpec((1, 8, rows), lambda p, _: (p, 0, 0)),
            whole(tables[0].shape),
            whole(tables[1].shape),
        ],
        [column] * 4,
        [struct((rows, width), BF16)] * 3 + [struct((rows, width), F32)],
        [pltpu.VMEM((PAIR, rows), F32)],
        "attend_back",
        20 * rows * rows * width,
        18 * rows * width,
        40,
    )(idx, queries, keys, values, grads, logs, *tables)


def gate_body(count, idx, attended, tokens, gains, own_out, own_gate, own_up, *rest):
    pieces, rest = rest[: 2 * count - 2], rest[2 * count - 2 :]
    (after, hidden_two, hidden_t, gate, up, product, product_t) = rest[:7]
    w_out, w_gate, w_up, sems = rest[7:]
    mine, other = pieces[: count - 1], pieces[count - 1 :]
    rows = own_out.shape[0]
    per = 2 * count - 1

    @pl.when(pl.program_id(0) == 0)
    def _():
        side_out, side = own_out.shape[1] // 2, own_gate.shape[1] // 2
        load = functools.partial(piece_copies, idx, rows=rows, count=count, sems=sems)
        first = load(own_out, mine, other, w_out, first=0, column=0, width=side_out)
        second = load(own_gate, mine, other, w_gate, first=per, column=side_out, width=side)
        third = load(own_up, mine, other, w_up, first=2 * per, column=side_out + side, width=side)
        start(first + second + third)
        wait(first)

        @pl.loop(0, w_out.shape[1] // TILE)
        def _(t):
            at = pl.multiple_of(t * TILE, TILE)
            after[:, pl.ds(at, TILE)] = tokens[:, pl.ds(at, TILE)].astype(F32) + dot_nn(
                attended[...], w_out[:, pl.ds(at, TILE)]
            )

        x = after[...]
        inverse = lax.rsqrt(jnp.mean(x * x, axis=-1, keepdims=True) + norm_eps)
        low = (x * inverse * gains[1:2, :]).astype(BF16)
        hidden_two[...] = low
        hidden_t[...] = low.T
        wait(second + third)

    at = pl.multiple_of(pl.program_id(0) * TILE, TILE)
    gate_pre = dot_nn(hidden_two[...], w_gate[:, pl.ds(at, TILE)])
    up_proj = dot_nn(hidden_two[...], w_up[:, pl.ds(at, TILE)])
    low = (gate_pre * jax.nn.sigmoid(gate_pre) * up_proj).astype(BF16)
    gate[...] = gate_pre.astype(gate.dtype)
    up[...] = up_proj.astype(up.dtype)
    product[...] = low
    product_t[...] = low.T


def gate_kernel(lay, idx, attended, tokens, gains, own_out, own_gate, own_up, mine, other):
    count = lay.fs
    rows, width = tokens.shape
    hidden = own_gate.shape[1]
    tile = pl.BlockSpec((rows, TILE), lambda t, _: (0, t))
    return call(
        functools.partial(gate_body, count),
        (hidden // TILE,),
        [whole(attended.shape), whole(tokens.shape), whole(gains.shape)] + [ANY] * (2 * count + 1),
        [
            whole((rows, width)),
            whole((rows, width)),
            whole((width, rows)),
            tile,
            tile,
            tile,
            pl.BlockSpec((TILE, rows), lambda t, _: (t, 0)),
        ],
        [
            struct((rows, width), F32),
            struct((rows, width), BF16),
            struct((width, rows), BF16),
            struct((rows, hidden), BF16),
            struct((rows, hidden), BF16),
            struct((rows, hidden), BF16),
            struct((hidden, rows), BF16),
        ],
        [
            pltpu.VMEM((width, width), BF16),
            pltpu.VMEM((width, hidden), BF16),
            pltpu.VMEM((width, hidden), BF16),
            pltpu.SemaphoreType.DMA((3 * (2 * count - 1),)),
        ],
        "gate",
        2 * rows * width * (width + 2 * hidden),
        2 * width * (width + 2 * hidden) + 8 * rows * hidden,
    )(idx, attended, tokens, gains, own_out, own_gate, own_up, *mine, *other)


def down_body(count, idx, cotangent, after, gate, up, product, own, *rest):
    pieces, rest = rest[: 2 * count - 2], rest[2 * count - 2 :]
    grad_gate, grad_up, output, weight, total, sems = rest
    mine, other = pieces[: count - 1], pieces[count - 1 :]
    t = pl.program_id(0)

    @pl.when(t == 0)
    def _():
        copies = piece_copies(
            idx, own, mine, other, weight, sems, 0, 0, own.shape[1] // 2, own.shape[0], count
        )
        start(copies)
        total[...] = after[...]
        wait(copies)

    rows_of = weight[pl.ds(pl.multiple_of(t * TILE, TILE), TILE), :]
    grad_product = dot_nt(cotangent[...], rows_of)
    gate_pre = gate[...].astype(F32)
    up_proj = up[...].astype(F32)
    sigma = jax.nn.sigmoid(gate_pre)
    grad_gate[...] = (
        grad_product * up_proj * sigma * (1.0 + gate_pre * (1.0 - sigma))
    ).astype(BF16)
    grad_up[...] = (grad_product * (gate_pre * sigma)).astype(BF16)
    total[...] += dot_nn(product[...], rows_of)

    @pl.when(t == pl.num_programs(0) - 1)
    def _():
        output[...] = total[...].astype(BF16)


def down_kernel(lay, idx, cotangent, after, gate, up, product, own, mine, other):
    count = lay.fs
    rows, width = cotangent.shape
    hidden = gate.shape[1]
    tile = pl.BlockSpec((rows, TILE), lambda t, _: (0, t))
    return call(
        functools.partial(down_body, count),
        (hidden // TILE,),
        [whole(cotangent.shape), whole(after.shape), tile, tile, tile] + [ANY] * (2 * count - 1),
        [tile, tile, whole((rows, width))],
        [
            struct((rows, hidden), BF16),
            struct((rows, hidden), BF16),
            struct((rows, width), BF16),
        ],
        [
            pltpu.VMEM((hidden, width), BF16),
            pltpu.VMEM((rows, width), F32),
            pltpu.SemaphoreType.DMA((2 * count - 1,)),
        ],
        "down",
        4 * rows * width * hidden,
        2 * width * hidden + 10 * rows * hidden,
    )(idx, cotangent, after, gate, up, product, own, *mine, *other)


def rms_back(grad, normed, inverse):
    return inverse * (grad - normed * jnp.mean(grad * normed, axis=-1, keepdims=True))


def mlp_back_body(count, idx, grad_gate, grad_up, after, cotangent, gains, own_out, own_gate, own_up, *rest):
    pieces, rest = rest[: 2 * count - 2], rest[2 * count - 2 :]
    grad_after, grad_low, grad_attended, grad_gain = rest[:4]
    w_out, w_gate, w_up, total, sems = rest[4:]
    mine, other = pieces[: count - 1], pieces[count - 1 :]
    rows = own_out.shape[0]
    per = 2 * count - 1
    side_out, side = own_out.shape[1] // 2, own_gate.shape[1] // 2
    load = functools.partial(piece_copies, idx, rows=rows, count=count, sems=sems)
    first = load(own_out, mine, other, w_out, first=0, column=0, width=side_out)
    second = load(own_gate, mine, other, w_gate, first=per, column=side_out, width=side)
    third = load(own_up, mine, other, w_up, first=2 * per, column=side_out + side, width=side)
    start(second + third + first)
    wait(second + third)
    width = w_gate.shape[0]

    @pl.loop(0, width // TILE)
    def _(t):
        at = pl.multiple_of(t * TILE, TILE)
        total[:, pl.ds(at, TILE)] = dot_nt(grad_gate[...], w_gate[pl.ds(at, TILE), :]) + dot_nt(
            grad_up[...], w_up[pl.ds(at, TILE), :]
        )

    x = after[...]
    inverse = lax.rsqrt(jnp.mean(x * x, axis=-1, keepdims=True) + norm_eps)
    normed = x * inverse
    grad_hidden = total[...]
    grad_gain[...] = jnp.zeros(grad_gain.shape, F32)
    grad_gain[0:1, :] = jnp.sum(grad_hidden * normed, axis=0, keepdims=True)
    result = cotangent[...].astype(F32) + rms_back(grad_hidden * gains[1:2, :], normed, inverse)
    grad_after[...] = result
    grad_low[...] = result.astype(BF16)
    wait(first)

    @pl.loop(0, width // TILE)
    def _(t):
        at = pl.multiple_of(t * TILE, TILE)
        grad_attended[:, pl.ds(at, TILE)] = dot_nt(
            grad_low[...], w_out[pl.ds(at, TILE), :]
        ).astype(BF16)


def mlp_back_kernel(lay, idx, grad_gate, grad_up, after, cotangent, gains, own_out, own_gate, own_up, mine, other):
    count = lay.fs
    rows, width = cotangent.shape
    hidden = grad_gate.shape[1]
    return call(
        functools.partial(mlp_back_body, count),
        (1,),
        [whole(grad_gate.shape), whole(grad_up.shape), whole(after.shape), whole(cotangent.shape), whole(gains.shape)]
        + [ANY] * (2 * count + 1),
        [whole((rows, width)), whole((rows, width)), whole((rows, width)), whole((8, width))],
        [
            struct((rows, width), F32),
            struct((rows, width), BF16),
            struct((rows, width), BF16),
            struct((8, width), F32),
        ],
        [
            pltpu.VMEM((width, width), BF16),
            pltpu.VMEM((width, hidden), BF16),
            pltpu.VMEM((width, hidden), BF16),
            pltpu.VMEM((rows, width), F32),
            pltpu.SemaphoreType.DMA((3 * (2 * count - 1),)),
        ],
        "mlp_back",
        2 * rows * width * (width + 2 * hidden),
        2 * width * (width + 2 * hidden) + 4 * rows * hidden + 12 * rows * width,
    )(idx, grad_gate, grad_up, after, cotangent, gains, own_out, own_gate, own_up, *mine, *other)


def qkv_back_body(count, idx, grad_q, grad_k, grad_v, tokens, grad_after, gains, own, *rest):
    pieces, rest = rest[: 2 * count - 2], rest[2 * count - 2 :]
    grad_tokens, grad_gain, weight, total, sems = rest
    mine, other = pieces[: count - 1], pieces[count - 1 :]
    copies = piece_copies(
        idx, own, mine, other, weight, sems, 0, 0, own.shape[1] // 2, own.shape[0], count
    )
    start(copies)
    x = tokens[...].astype(F32)
    inverse = lax.rsqrt(jnp.mean(x * x, axis=-1, keepdims=True) + norm_eps)
    width = weight.shape[0]
    wait(copies)

    @pl.loop(0, width // TILE)
    def _(t):
        at = pl.multiple_of(t * TILE, TILE)
        block = pl.ds(at, TILE)
        total[:, block] = (
            dot_nt(grad_q[...], weight[block, 0:width])
            + dot_nt(grad_k[...], weight[block, width : 2 * width])
            + dot_nt(grad_v[...], weight[block, 2 * width : 3 * width])
        )

    normed = x * inverse
    grad_hidden = total[...]
    grad_gain[...] = jnp.zeros(grad_gain.shape, F32)
    grad_gain[0:1, :] = jnp.sum(grad_hidden * normed, axis=0, keepdims=True)
    grad_tokens[...] = grad_after[...] + rms_back(grad_hidden * gains[0:1, :], normed, inverse)


def qkv_back_kernel(lay, idx, grad_q, grad_k, grad_v, tokens, grad_after, gains, own, mine, other):
    count = lay.fs
    rows, width = tokens.shape
    n = own.shape[1]
    operands = (grad_q, grad_k, grad_v, tokens, grad_after, gains)
    return call(
        functools.partial(qkv_back_body, count),
        (1,),
        [whole(item.shape) for item in operands] + [ANY] * (2 * count - 1),
        [whole((rows, width)), whole((8, width))],
        [struct((rows, width), F32), struct((8, width), F32)],
        [
            pltpu.VMEM((width, n), BF16),
            pltpu.VMEM((rows, width), F32),
            pltpu.SemaphoreType.DMA((2 * count - 1,)),
        ],
        "qkv_back",
        2 * rows * width * n,
        2 * width * n + 16 * rows * width,
    )(idx, *operands, own, *mine, *other)


def grad_sibling_body(parts, idx, turned, *rest):
    lefts, out = rest[:parts], rest[parts]
    side = lefts[0].shape[1]
    for i, left in enumerate(lefts):
        out[0, :, i * side : (i + 1) * side] = dot_nn(turned[...], left[...]).astype(BF16)


def grad_own_body(parts, blocks, idx, turned, *rest):
    lefts, got, keep, send = rest[:parts], rest[parts], rest[parts + 1], rest[parts + 2]
    side = lefts[0].shape[1]
    place = pl.program_id(0)

    def block(out):
        for i, left in enumerate(lefts):
            columns = slice(i * side, (i + 1) * side)
            summed = dot_nn(turned[...], left[...]) + got[0, :, columns].astype(F32)
            out[0, :, columns] = summed.astype(BF16)

    @pl.when(place < blocks // 2)
    def _():
        block(keep)

    @pl.when(place >= blocks // 2)
    def _():
        block(send)


def weight_grad(lay, idx, turned, lefts, name):
    blocks = lay.fs
    total, rows = turned.shape
    block = total // blocks
    half = [left.shape[1] // 2 for left in lefts]
    wide = sum(half)
    cost = (2 * rows * total * wide, 2 * rows * (total + wide) + 2 * total * wide)
    base = IDX_HEAD + 2 * blocks

    def shard(p, idx):
        return (idx[base + p], 0)

    sibling = call(
        functools.partial(grad_sibling_body, len(lefts)),
        (blocks,),
        [pl.BlockSpec((block, rows), lambda p, idx: (p, 0))]
        + [pl.BlockSpec((rows, side), lambda p, idx: (0, idx[1])) for side in half],
        [pl.BlockSpec((1, block, wide), lambda p, idx: (p, 0, 0))],
        [struct((blocks, block, wide), BF16)],
        [],
        name + "_sibling",
        *cost,
    )(idx, turned, *lefts)[0]
    got = lay.core(sibling)
    return call(
        functools.partial(grad_own_body, len(lefts), blocks),
        (blocks,),
        [pl.BlockSpec((block, rows), shard)]
        + [pl.BlockSpec((rows, side), lambda p, idx: (0, idx[0])) for side in half]
        + [pl.BlockSpec((1, block, wide), lambda p, idx: (idx[base + p], 0, 0))],
        [
            pl.BlockSpec((1, block, wide), lambda p, idx: (jnp.minimum(p, blocks // 2 - 1), 0, 0)),
            pl.BlockSpec((1, block, wide), lambda p, idx: (jnp.maximum(p - blocks // 2, 0), 0, 0)),
        ],
        [struct((blocks // 2, block, wide), BF16)] * 2,
        [],
        name + "_own",
        *cost,
    )(idx, turned, *lefts, got)


def finish_body(parts, idx, mine, other, *outs):
    low = idx[0] == 0
    at = 0
    for out in outs:
        side = out.shape[1] // 2
        a = mine[:, at : at + side].astype(F32)
        b = other[:, at : at + side].astype(F32)
        out[:, 0:side] = jnp.where(low, a, b)
        out[:, side:] = jnp.where(low, b, a)
        at += side


def finish(lay, idx, mine, widths, name):
    other = lay.core(mine)
    rows, wide = mine.shape
    block = rows // 4 if rows % 64 == 0 else rows
    return call(
        functools.partial(finish_body, len(widths)),
        (rows // block,),
        [pl.BlockSpec((block, wide), lambda p, _: (p, 0))] * 2,
        [pl.BlockSpec((block, 2 * side), lambda p, _: (p, 0)) for side in widths],
        [struct((rows, 2 * side), F32) for side in widths],
        [],
        name,
        0,
        12 * rows * wide,
    )(idx, mine, other)


def body(
    lay,
    tokens,
    first_values,
    lengths,
    gain_one,
    w_qkv,
    w_out,
    gain_two,
    w_gate,
    w_up,
    w_down,
    cotangent,
):
    rows, width = tokens.shape
    hidden = w_gate.shape[1]
    shard_rows = w_qkv.shape[0]
    idx = lay.index(lengths[0])
    tables = tuple(jnp.asarray(table) for table in rotary_tables(rows))
    c = lax.axis_index("dp") % 2

    def half_of(weight):
        side = weight.shape[1] // 2
        return lax.dynamic_slice_in_dim(weight, c * side, side, axis=1)

    gain_block = jnp.concatenate([gain_one, gain_two])
    half_qkv = half_of(w_qkv)
    gain_block = jnp.pad(
        gain_block[None], ((0, GAIN_ROWS - 1), (0, half_qkv.shape[1] - 2 * shard_rows))
    )
    half_a = jnp.concatenate([half_qkv, gain_block], axis=0)
    half_b = jnp.concatenate([half_of(w_out), half_of(w_gate), half_of(w_up)], axis=1)
    half_c = half_of(w_down)
    mine_a, other_a = lay.gather(half_a)
    mine_b, other_b = lay.gather(half_b)
    mine_c, other_c = lay.gather(half_c)

    queries, keys, values, hidden_one_t, gains, sums = qkv_kernel(
        lay, idx, tokens, first_values, tables, w_qkv, half_a, mine_a[1:], other_a
    )
    attended, attended_t, logs = attend_kernel(idx, queries, keys, values)
    after, hidden_two, hidden_two_t, gate, up, product, product_t = gate_kernel(
        lay, idx, attended, tokens, gains, w_out, w_gate, w_up, mine_b[1:], other_b
    )
    keep, send = weight_grad(lay, idx, product_t, [cotangent], "grad_down")
    total_down = lay.reduce(keep, send)
    grad_gate, grad_up, output = down_kernel(
        lay, idx, cotangent, after, gate, up, product, w_down, mine_c[1:], other_c
    )
    keep, send = weight_grad(lay, idx, hidden_two_t, [grad_gate, grad_up], "grad_gate_up")
    total_gate_up = lay.reduce(keep, send)
    grad_after, grad_after_low, grad_attended, grad_gain_two = mlp_back_kernel(
        lay, idx, grad_gate, grad_up, after, cotangent, gains, w_out, w_gate, w_up, mine_b[1:], other_b
    )
    keep, send = weight_grad(lay, idx, attended_t, [grad_after_low], "grad_out")
    total_out = lay.reduce(keep, send)
    grad_q, grad_k, grad_v, grad_first = attend_back_kernel(
        idx, queries, keys, values, grad_attended, logs, tables
    )
    keep, send = weight_grad(lay, idx, hidden_one_t, [grad_q, grad_k, grad_v], "grad_qkv")
    total_qkv = lay.reduce(keep, send)
    grad_tokens, grad_gain_one = qkv_back_kernel(
        lay, idx, grad_q, grad_k, grad_v, tokens, grad_after, gains, w_qkv, mine_a[1:], other_a
    )

    small = jnp.concatenate(
        [
            grad_gain_one[0:1],
            grad_gain_two[0:1],
            jnp.pad(jnp.sum(sums, axis=1)[None], ((0, 5), (0, width - 8))),
        ]
    )
    small = lay.small_sum(small)
    at = lax.axis_index("fsdp") * shard_rows
    entry_count = rows * width * lay.dp * lay.fs
    shard_gain_one = lax.dynamic_slice(small[0], (at,), (shard_rows,))
    shard_gain_two = lax.dynamic_slice(small[1], (at,), (shard_rows,))
    first_norm = small[2, 0] / entry_count
    value_norm = small[2, 1] / entry_count

    (shard_down,) = finish(lay, idx, total_down, [width // 2], "finish_down")
    shard_gate, shard_up = finish(lay, idx, total_gate_up, [hidden // 2] * 2, "finish_gate_up")
    (shard_out,) = finish(lay, idx, total_out, [width // 2], "finish_out")
    third = width // 2
    other_qkv = lay.core(total_qkv)
    low = c == 0
    blocks = []
    for i in range(3):
        a = total_qkv[:, i * third : (i + 1) * third].astype(F32)
        b = other_qkv[:, i * third : (i + 1) * third].astype(F32)
        blocks += [jnp.where(low, a, b), jnp.where(low, b, a)]
    shard_qkv = jnp.concatenate(blocks, axis=1)
    return (
        output,
        grad_tokens,
        grad_first,
        shard_gain_one,
        shard_qkv,
        shard_out,
        shard_gain_two,
        shard_gate,
        shard_up,
        shard_down,
        first_norm,
        value_norm,
    )


def solution(mesh):
    both = P(AXES, None)
    rows = P("fsdp", None)
    in_specs = (both, both, P(AXES), P("fsdp"), rows, rows, P("fsdp"), rows, rows, rows, both)
    out_specs = (both, both, both, P("fsdp"), rows, rows, P("fsdp"), rows, rows, rows, P(), P())
    lay = Layout(mesh.shape["dp"], mesh.shape["fsdp"])
    return jax.shard_map(
        functools.partial(body, lay),
        mesh=mesh,
        in_specs=in_specs,
        out_specs=out_specs,
        check_vma=False,
    )
```

time: 1600 us -> 540 us (0.34)
  waiting for transfers between devices: 1210 us -> 240 us
  Pallas kernels: 0 us -> 187 us
  matrix products: 147 us -> 0 us
  blocking collectives: 91.5 us -> 0 us
  starting transfers between devices: 0.82 us -> 54 us
  other arithmetic: 58.7 us -> 19.9 us
  local copies, waits for them, and re-layouts: 59.5 us -> 29.5 us
    reduce_scatter x5 -> x0, waiting for transfers between devices: 902 us -> none  [the longest x1 251 us: body(): lax.psum_scatter(reorder_rows(grad_w_gate, owners, replicas), ('dp', 'fsd...]
    all_gather x9 -> x0, waiting for transfers between devices: 308 us -> none  [the longest x1 62.9 us: body(): lax.all_gather(w_up, 'fsdp', axis=0, tiled=True)]
    ppermute x0 -> x51, waiting for transfers between devices: none -> 240 us  [send(): return lax.ppermute(x, AXES, self.perm(move))]
    pallas_call x0 -> x18, Pallas kernels: none -> 187 us  [the longest x4 28.3 us: weight_grad(): call(functools.partial(grad_own_body, len(lefts), blocks), (blocks,), [pl...]
    dot_general x21 -> x0, matrix products: 147 us -> none  [the longest x1 14.6 us: body(): jnp.einsum('qhd,khd->hqk', grad_attended, values_low, preferred_element_t...]
    unnamed x2 -> x0, blocking collectives: 57.8 us -> none
    ppermute x0 -> x51, starting transfers between devices: none -> 54 us  [send(): return lax.ppermute(x, AXES, self.perm(move))]
    transpose x7 -> x0, local copies, waits for them, and re-layouts: 46.4 us -> none  [reorder_rows(): return jnp.swapaxes(shaped, 0, 1).reshape(grad.shape)]
  transfers between devices with their start and end apart: 14 -> 51, of which waited for: 14 -> 13; matrix products, arithmetic and copies ran while one was open for 10% -> 5% of each run, Pallas kernels for 0% -> 29%
where the time goes in v1:
time: 540 us; the launch traced here: 537 us
  waiting for transfers between devices  240 us (44%)
  Pallas kernels  187 us (35%)
  starting transfers between devices  54 us (10%)
  local copies, waits for them, and re-layouts  29.5 us (5%)
  other arithmetic  19.9 us (4%)
  between operations  5.65 us (1%)
    ppermute x51, waiting for transfers between devices, send(): return lax.ppermute(x, AXES, self.perm(move))  240 us
    ppermute x51, starting transfers between devices, send(): return lax.ppermute(x, AXES, self.perm(move))  54 us
    pallas_call x4, Pallas kernels, weight_grad(): call(functools.partial(grad_own_body, len(lefts), blocks), (blocks,), [pl...  28.3 us
    pallas_call x4, Pallas kernels, weight_grad(): call(functools.partial(grad_sibling_body, len(lefts)), (blocks,), [pl.Blo...  24.9 us
    pallas_call x1, Pallas kernels, attend_back_kernel(): call(attend_back_body, (pairs,), [column] * 4 + [pl.BlockSpec((1, 8, rows...  20.4 us
    pallas_call x1, Pallas kernels, mlp_back_kernel(): call(functools.partial(mlp_back_body, count), (1,), [whole(grad_gate.shap...  20.2 us
    pallas_call x1, Pallas kernels, down_kernel(): call(functools.partial(down_body, count), (hidden // TILE,), [whole(cotan...  18.5 us
    unnamed x88, local copies, waits for them, and re-layouts  18.3 us
  transfers between devices with their start and end apart: 51, of which 13 were waited for; matrix products, arithmetic and copies ran while one was open for 5% of the time, Pallas kernels for 29%

profile of v1, /device:TPU:0, one launch (start us, length us, event | category | flops | bytes accessed | tf_op | source)
XLA Modules:
  0.0 536.6 jit_solution(3754264401182480272)
XLA Ops:
  9.2 34.6 %collective-permute-done.6.rest_0_ = bf16[256,3328]{1,0:T(8,128)(2,1)} collective-permute-done((bf16[256,3328]{1,0:T(8,128)(2,1)S(1)}, bf16[256,3328]{1,0:T(8,128)(2,1)}, u32[]{:S(2)}, u32[]{:S(2)}) %collective-permute-start.6) | collective-permute-done | bytes 1703968 | tf_op jit(solution)/shard_map/ppermute | solution.py:76
  46.5 14.9 %collective-permute-done.1.rest_2_.rest_1_ = bf16[272,1536]{1,0:T(8,128)(2,1)S(1)} collective-permute-done((bf16[272,1536]{1,0:T(8,128)(2,1)S(1)}, bf16[272,1536]{1,0:T(8,128)(2,1)S(1)}, u32[]{:S(2)}, u32[]{:S(2)}) %collective-permute-start.1) | collective-permute-done | bytes 835616 | tf_op jit(solution)/shard_map/ppermute | solution.py:76
  66.7 17.9 %collective-permute-done.12.rest_0_ = bf16[704,512]{1,0:T(8,128)(2,1)} collective-permute-done((bf16[704,512]{1,0:T(8,128)(2,1)}, bf16[704,512]{1,0:T(8,128)(2,1)}, u32[]{:S(2)}, u32[]{:S(2)}) %collective-permute-start.12) | collective-permute-done | bytes 720928 | tf_op jit(solution)/shard_map/ppermute | solution.py:76
  84.6 11.7 %collective-permute-done.2.rest_3_.rest_2_ = bf16[272,1536]{1,0:T(8,128)(2,1)S(1)} collective-permute-done((bf16[272,1536]{1,0:T(8,128)(2,1)S(1)}, bf16[272,1536]{1,0:T(8,128)(2,1)S(1)}, u32[]{:S(2)}, u32[]{:S(2)}) %collective-permute-start.2) | collective-permute-done | bytes 835616 | tf_op jit(solution)/shard_map/ppermute | solution.py:76
  101.7 14.8 %qkv.1 = (bf16[512,1024]{1,0:T(8,128)(2,1)}, bf16[512,1024]{1,0:T(8,128)(2,1)}, bf16[512,1024]{1,0:T(8,128)(2,1)}, bf16[1024,512]{1,0:T(8,128)(2,1)}, f32[8,1024]{1,0:T(8,128)}, /*index=5*/f32[8,256]{1,0:T(8,128)}) custom-call(s32[16]{0:T(128)} %concatenate.18.idx, bf16[512,1024]{1,0:T(8,128)(2,1)} %tokens.5, bf16[512,1024]{1,0:T(8,128)(2,1)} %first.1, ...), custom_call_target="tpu_custom_call" | custom-call | flops 3221225472 | bytes 12582912 | tf_op jit(solution)/shard_map/qkv/pallas_call | solution.py:280
  121.7 15.8 %attend.1 = (bf16[512,1024]{1,0:T(8,128)(2,1)S(1)}, bf16[1024,512]{1,0:T(8,128)(2,1)S(1)}, f32[8,8,512]{2,1,0:T(8,128)S(1)}) custom-call(s32[16]{0:T(128)S(1)} %copy-done.4, bf16[512,1024]{1,0:T(8,128)(2,1)S(1)} %copy-done.8, bf16[512,1024]{1,0:T(8,128)(2,1)S(1)} %copy-done.10, bf16[512,1024]{1,0:T(8,128)(2,1)S(1)} %copy-done.12), custom_call_target="tpu_custom_call" | custom-call | flops 2147483648 | bytes 5242880 | tf_op jit(solution)/shard_map/attend/pallas_call | solution.py:348
  139.5 18.1 %gate.1 = (f32[512,1024]{1,0:T(8,128)}, bf16[512,1024]{1,0:T(8,128)(2,1)}, bf16[1024,512]{1,0:T(8,128)(2,1)}, bf16[512,2816]{1,0:T(8,128)(2,1)}, bf16[512,2816]{...) custom-call(s32[16]{0:T(128)} %concatenate.18.idx, bf16[512,1024]{1,0:T(8,128)(2,1)} %copy-done.15, ...), custom_call_target="tpu_custom_call" | custom-call | flops 6979321856 | bytes 25165824 | tf_op jit(solution)/shard_map/gate/pallas_call | solution.py:495
  159.0 18.5 %down.1 = (bf16[512,2816]{1,0:T(8,128)(2,1)}, bf16[512,2816]{1,0:T(8,128)(2,1)}, bf16[512,1024]{1,0:T(8,128)(2,1)}) custom-call(s32[16]{0:T(128)} %concatenate.18.idx, bf16[512,1024]{1,0:T(8,128)(2,1)} %rest_0_.3, f32[512,1024]{1,0:T(8,128)} %get-tuple-element.55.after, bf16[512,2816]{1,0:T(8,128)(2,1)} %get-tuple-element.56.gate, ...), custom_call_target="tpu_custom_call" | custom-call | flops 5905580032 | bytes 20185088 | tf_op jit(solution)/shard_map/down/pallas_call | solution.py:565
  177.5 7.9 %grad_gate_up_sibling.1 = bf16[4,256,2816]{2,1,0:T(8,128)(2,1)} custom-call(s32[16]{0:T(128)} %concatenate.18.idx, bf16[1024,512]{1,0:T(8,128)(2,1)} %get-tuple-element.80.turned, bf16[512,2816]{1,0:T(8,128)(2,1)} %get-tuple-element.60.grad_gate.rest_0_, bf16[512,2816]{1,0:T(8,128)(2,1)} %get-tuple-element.61.grad_up.rest_1_), custom_call_target="tpu_custom_call" | custom-call | flops 2952790016 | bytes 9699328 | tf_op jit(solution)/shard_map/grad_gate_up_sibling/pallas_call | solution.py:752
  185.6 20.2 %mlp_back.1 = (f32[512,1024]{1,0:T(8,128)}, bf16[512,1024]{1,0:T(8,128)(2,1)}, bf16[512,1024]{1,0:T(8,128)(2,1)}, f32[8,1024]{1,0:T(8,128)}) custom-call(s32[16]{0:T(128)} %concatenate.18.idx, bf16[512,2816]{1,0:T(8,128)(2,1)} %get-tuple-element.60.grad_gate.rest_0_, bf16[512,2816]{1,0:T(8,128)(2,1)} %get-tuple-element.61.grad_up.rest_1_, ...), custom_call_target="tpu_custom_call" | custom-call | flops 6979321856 | bytes 25690112 | tf_op jit(solution)/shard_map/mlp_back/pallas_call | solution.py:636
  207.1 20.4 %attend_back.1 = (bf16[512,1024]{1,0:T(8,128)(2,1)S(1)}, bf16[512,1024]{1,0:T(8,128)(2,1)S(1)}, bf16[512,1024]{1,0:T(8,128)(2,1)S(1)}, f32[512,1024]{1,0:T(8,128)}) custom-call(s32[16]{0:T(128)S(1)} %copy-done.5, bf16[512,1024]{1,0:T(8,128)(2,1)S(1)} %copy-done.9, bf16[512,1024]{1,0:T(8,128)(2,1)S(1)} %copy-done.11, bf16[512,1024]{1,0:T(8,128)(2,1)S(1)} %copy-done.13, ...), custom_call_target="tpu_custom_call" | custom-call | flops 5368709120 | bytes 9437184 | tf_op jit(solution)/shard_map/attend_back/pallas_call | solution.py:429
  236.8 6.1 %grad_down_sibling.1 = bf16[4,704,512]{2,1,0:T(8,128)(2,1)} custom-call(s32[16]{0:T(128)} %concatenate.18.idx, bf16[2816,512]{1,0:T(8,128)(2,1)} %get-tuple-element.85.turned, bf16[512,1024]{1,0:T(8,128)(2,1)} %rest_0_.3), custom_call_target="tpu_custom_call" | custom-call | flops 1476395008 | bytes 6291456 | tf_op jit(solution)/shard_map/grad_down_sibling/pallas_call | solution.py:752
  243.1 9.6 %grad_gate_up_own.1 = (bf16[2,256,2816]{2,1,0:T(8,128)(2,1)}, bf16[2,256,2816]{2,1,0:T(8,128)(2,1)}) custom-call(s32[16]{0:T(128)} %concatenate.18.idx, bf16[1024,512]{1,0:T(8,128)(2,1)} %get-tuple-element.80.turned, bf16[512,2816]{1,0:T(8,128)(2,1)} %get-tuple-element.60.grad_gate.rest_0_, bf16[512,2816]{1,0:T(8,128)(2,1)} %get-tuple-element.61.grad_up.rest_1_, ...), custom_call_target="tpu_custom_call" | custom-call | flops 2952790016 | bytes 9699328 | tf_op jit(solution)/shard_map/grad_gate_up_own/pallas_call | solution.py:764
  255.3 12.6 %qkv_back.1 = (f32[512,1024]{1,0:T(8,128)}, f32[8,1024]{1,0:T(8,128)}) custom-call(s32[16]{0:T(128)} %concatenate.18.idx, bf16[512,1024]{1,0:T(8,128)(2,1)} %copy-done, bf16[512,1024]{1,0:T(8,128)(2,1)} %copy-done.1, bf16[512,1024]{1,0:T(8,128)(2,1)} %copy-done.2, bf16[512,1024]{1,0:T(8,128)(2,1)} %tokens.5, f32[512,1024]{1,0:T(8,128)} %get-tuple-element.67.grad_after, ...), custom_call_target="tpu_custom_call" | custom-call | flops 3221225472 | bytes 14680064 | tf_op jit(solution)/shard_map/qkv_back/pallas_call | solution.py:696
  274.1 6.7 %grad_down_own.1 = (bf16[2,704,512]{2,1,0:T(8,128)(2,1)}, bf16[2,704,512]{2,1,0:T(8,128)(2,1)}) custom-call(s32[16]{0:T(128)} %concatenate.18.idx, bf16[2816,512]{1,0:T(8,128)(2,1)} %get-tuple-element.85.turned, bf16[512,1024]{1,0:T(8,128)(2,1)} %rest_0_.3, bf16[4,704,512]{2,1,0:T(8,128)(2,1)} %collective-permute-done.44.rest_1_), custom_call_target="tpu_custom_call" | custom-call | flops 1476395008 | bytes 6291456 | tf_op jit(solution)/shard_map/grad_down_own/pallas_call | solution.py:764
  282.8 6.9 %grad_qkv_own.1 = (bf16[2,256,1536]{2,1,0:T(8,128)(2,1)}, bf16[2,256,1536]{2,1,0:T(8,128)(2,1)}) custom-call(s32[16]{0:T(128)} %concatenate.18.idx, bf16[1024,512]{1,0:T(8,128)(2,1)} %get-tuple-element.73.turned, bf16[512,1024]{1,0:T(8,128)(2,1)} %copy-done, bf16[512,1024]{1,0:T(8,128)(2,1)} %copy-done.1, bf16[512,1024]{1,0:T(8,128)(2,1)} %copy-done.2, ...), custom_call_target="tpu_custom_call" | custom-call | flops 1610612736 | bytes 5767168 | tf_op jit(solution)/shard_map/grad_qkv_own/pallas_call | solution.py:764
  297.5 37.9 %collective-permute-done.19 = f32[8,1024]{1,0:T(8,128)S(1)} collective-permute-done((f32[8,1024]{1,0:T(8,128)S(1)}, f32[8,1024]{1,0:T(8,128)S(1)}, u32[]{:S(2)}, u32[]{:S(2)}) %collective-permute-start.19) | collective-permute-done | bytes 32800 | tf_op jit(solution)/shard_map/ppermute | solution.py:76
  367.1 24.7 %collective-permute-done.22 = f32[8,1024]{1,0:T(8,128)} collective-permute-done((f32[8,1024]{1,0:T(8,128)}, f32[8,1024]{1,0:T(8,128)}, u32[]{:S(2)}, u32[]{:S(2)}) %collective-permute-start.22) | collective-permute-done | bytes 32800 | tf_op jit(solution)/shard_map/ppermute | solution.py:76
  393.6 6.5 %collective-permute-start.33 = (bf16[256,512]{1,0:T(8,128)(2,1)S(1)}, bf16[256,512]{1,0:T(8,128)(2,1)S(1)}, u32[]{:S(2)}, u32[]{:S(2)}) collective-permute-start(bf16[256,512]{1,0:T(8,128)(2,1)S(1)} %fusion.11), channel_id=1, source_target_pairs={{0,8},{1,9},{2,10},{3,11},{4,12},{5,13},{6,14},{7,15},{24,16},{25,... | collective-permute-start | bytes 786440 | tf_op jit(solution)/shard_map/ppermute | solution.py:76
  409.2 13.2 %collective-permute-done.47 = bf16[704,512]{1,0:T(8,128)(2,1)S(1)} collective-permute-done((bf16[704,512]{1,0:T(8,128)(2,1)S(1)}, bf16[704,512]{1,0:T(8,128)(2,1)S(1)}, u32[]{:S(2)}, u32[]{:S(2)}) %collective-permute-start.47) | collective-permute-done | bytes 720928 | tf_op jit(solution)/shard_map/ppermute | solution.py:76
  424.9 8.6 %collective-permute-done.26 = bf16[256,1536]{1,0:T(8,128)(2,1)S(1)} collective-permute-done((bf16[256,1536]{1,0:T(8,128)(2,1)S(1)}, bf16[256,1536]{1,0:T(8,128)(2,1)S(1)}, u32[]{:S(2)}, u32[]{:S(2)}) %collective-permute-start.26) | collective-permute-done | bytes 786464 | tf_op jit(solution)/shard_map/ppermute | solution.py:76
  441.0 13.7 %collective-permute-done.35 = bf16[256,512]{1,0:T(8,128)(2,1)S(1)} collective-permute-done((bf16[256,512]{1,0:T(8,128)(2,1)S(1)}, bf16[256,512]{1,0:T(8,128)(2,1)S(1)}, u32[]{:S(2)}, u32[]{:S(2)}) %collective-permute-start.35) | collective-permute-done | bytes 262176 | tf_op jit(solution)/shard_map/ppermute | solution.py:76
  454.8 28.1 %collective-permute-done.49 = bf16[704,512]{1,0:T(8,128)(2,1)S(1)} collective-permute-done((bf16[704,512]{1,0:T(8,128)(2,1)S(1)}, bf16[704,512]{1,0:T(8,128)(2,1)S(1)}, u32[]{:S(2)}, u32[]{:S(2)}) %collective-permute-start.49) | collective-permute-done | bytes 720928 | tf_op jit(solution)/shard_map/ppermute | solution.py:76
  488.9 29.7 %collective-permute-done.28 = bf16[256,1536]{1,0:T(8,128)(2,1)S(1)} collective-permute-done((bf16[256,1536]{1,0:T(8,128)(2,1)S(1)}, bf16[256,1536]{1,0:T(8,128)(2,1)S(1)}, u32[]{:S(2)}, u32[]{:S(2)}) %collective-permute-start.28) | collective-permute-done | bytes 786464 | tf_op jit(solution)/shard_map/ppermute | solution.py:76
  (237 shorter events, 131.7 us)
Async XLA Ops:
  3.3 40.6 %collective-permute-start.6 = (bf16[256,3328]{1,0:T(8,128)(2,1)S(1)}, bf16[256,3328]{1,0:T(8,128)(2,1)}, u32[]{:S(2)}, u32[]{:S(2)}) collective-permute-start(bf16[256,3328]{1,0:T(8,128)(2,1)S(1)} %pad_maximum_fusion), channel_id=1, source_target_pairs={{0,1},{1,0},{2,3},{3,2},{4,6},{5,7},{6,4},{7,5},{8,9},{9,8},{10,11... | collective-permute-start | bytes 5111816 | tf_op jit(solution)/shard_map/ppermute | solution.py:76
  6.3 60.4 %collective-permute-start.7 = (bf16[256,3328]{1,0:T(8,128)(2,1)S(1)}, bf16[256,3328]{1,0:T(8,128)(2,1)}, u32[]{:S(2)}, u32[]{:S(2)}) collective-permute-start(bf16[256,3328]{1,0:T(8,128)(2,1)S(1)} %pad_maximum_fusion), channel_id=1, source_target_pairs={{0,2},{1,3},{2,0},{3,1},{4,5},{5,4},{6,7},{7,6},{8,10},{9,11},{10,... | collective-permute-start | bytes 5111816 | tf_op jit(solution)/shard_map/ppermute | solution.py:76
  8.0 53.4 %collective-permute-start.1 = (bf16[272,1536]{1,0:T(8,128)(2,1)S(1)}, bf16[272,1536]{1,0:T(8,128)(2,1)S(1)}, u32[]{:S(2)}, u32[]{:S(2)}) collective-permute-start(bf16[272,1536]{1,0:T(8,128)(2,1)S(1)} %fusion.2.rest_0_), channel_id=1, source_target_pairs={{0,2},{1,3},{2,0},{3,1},{4,5},{5,4},{6,7},{7,6},{8,10},{9,11},{10,... | collective-permute-start | bytes 2506760 | tf_op jit(solution)/shard_map/ppermute | solution.py:76
  8.5 53.9 %collective-permute-start = (bf16[272,1536]{1,0:T(8,128)(2,1)S(1)}, bf16[272,1536]{1,0:T(8,128)(2,1)S(1)}, u32[]{:S(2)}, u32[]{:S(2)}) collective-permute-start(bf16[272,1536]{1,0:T(8,128)(2,1)S(1)} %fusion.2.rest_0_), channel_id=1, source_target_pairs={{0,1},{1,0},{2,3},{3,2},{4,6},{5,7},{6,4},{7,5},{8,9},{9,8},{10,11... | collective-permute-start | bytes 2506760 | tf_op jit(solution)/shard_map/ppermute | solution.py:76
  43.8 53.2 %collective-permute-start.8 = (bf16[256,3328]{1,0:T(8,128)(2,1)}, bf16[256,3328]{1,0:T(8,128)(2,1)}, u32[]{:S(2)}, u32[]{:S(2)}) collective-permute-start(bf16[256,3328]{1,0:T(8,128)(2,1)} %collective-permute-done.6.rest_0_), channel_id=1, source_target_pairs={{0,2},{1,3},{2,0},{3,1},{4,5},{5,4},{6,7},{7,6},{8,10},{9,11},{10,... | collective-permute-start | bytes 5111816 | tf_op jit(solution)/shard_map/ppermute | solution.py:76
  66.7 50.9 %collective-permute-start.10 = (bf16[256,3328]{1,0:T(8,128)(2,1)}, bf16[256,3328]{1,0:T(8,128)(2,1)}, u32[]{:S(2)}, u32[]{:S(2)}) collective-permute-start(bf16[256,3328]{1,0:T(8,128)(2,1)} %collective-permute-done.7.rest_1_), channel_id=1, source_target_pairs={{0,4},{1,5},{2,6},{3,7},{4,0},{5,1},{6,2},{7,3},{8,12},{9,13},{10,... | collective-permute-start | bytes 5111816 | tf_op jit(solution)/shard_map/ppermute | solution.py:76
  97.0 42.5 %collective-permute-start.9 = (bf16[256,3328]{1,0:T(8,128)(2,1)}, bf16[256,3328]{1,0:T(8,128)(2,1)}, u32[]{:S(2)}, u32[]{:S(2)}) collective-permute-start(bf16[256,3328]{1,0:T(8,128)(2,1)} %collective-permute-done.6.rest_0_), channel_id=1, source_target_pairs={{0,4},{1,5},{2,6},{3,7},{4,0},{5,1},{6,2},{7,3},{8,12},{9,13},{10,... | collective-permute-start | bytes 5111816 | tf_op jit(solution)/shard_map/ppermute | solution.py:76
  97.1 42.4 %collective-permute-start.11 = (bf16[256,3328]{1,0:T(8,128)(2,1)}, bf16[256,3328]{1,0:T(8,128)(2,1)}, u32[]{:S(2)}, u32[]{:S(2)}) collective-permute-start(bf16[256,3328]{1,0:T(8,128)(2,1)} %collective-permute-done.8.rest_2_), channel_id=1, source_target_pairs={{0,4},{1,5},{2,6},{3,7},{4,0},{5,1},{6,2},{7,3},{8,12},{9,13},{10,... | collective-permute-start | bytes 5111816 | tf_op jit(solution)/shard_map/ppermute | solution.py:76
  116.6 41.1 %collective-permute-start.15 = (bf16[704,512]{1,0:T(8,128)(2,1)}, bf16[704,512]{1,0:T(8,128)(2,1)S(1)}, u32[]{:S(2)}, u32[]{:S(2)}) collective-permute-start(bf16[704,512]{1,0:T(8,128)(2,1)} %collective-permute-done.12.rest_0_), channel_id=1, source_target_pairs={{0,4},{1,5},{2,6},{3,7},{4,0},{5,1},{6,2},{7,3},{8,12},{9,13},{10,... | collective-permute-start | bytes 2162696 | tf_op jit(solution)/shard_map/ppermute | solution.py:76
  117.5 40.1 %collective-permute-start.16 = (bf16[704,512]{1,0:T(8,128)(2,1)S(1)}, bf16[704,512]{1,0:T(8,128)(2,1)S(1)}, u32[]{:S(2)}, u32[]{:S(2)}) collective-permute-start(bf16[704,512]{1,0:T(8,128)(2,1)S(1)} %collective-permute-done.13.rest_1_), channel_id=1, source_target_pairs={{0,4},{1,5},{2,6},{3,7},{4,0},{5,1},{6,2},{7,3},{8,12},{9,13},{10,... | collective-permute-start | bytes 2162696 | tf_op jit(solution)/shard_map/ppermute | solution.py:76
  117.6 40.1 %collective-permute-start.17 = (bf16[704,512]{1,0:T(8,128)(2,1)}, bf16[704,512]{1,0:T(8,128)(2,1)S(1)}, u32[]{:S(2)}, u32[]{:S(2)}) collective-permute-start(bf16[704,512]{1,0:T(8,128)(2,1)} %collective-permute-done.14.rest_2_), channel_id=1, source_target_pairs={{0,4},{1,5},{2,6},{3,7},{4,0},{5,1},{6,2},{7,3},{8,12},{9,13},{10,... | collective-permute-start | bytes 2162696 | tf_op jit(solution)/shard_map/ppermute | solution.py:76
  185.4 57.6 %collective-permute-start.37 = (bf16[4,256,2816]{2,1,0:T(8,128)(2,1)}, bf16[4,256,2816]{2,1,0:T(8,128)(2,1)}, u32[]{:S(2)}, u32[]{:S(2)}) collective-permute-start(bf16[4,256,2816]{2,1,0:T(8,128)(2,1)} %grad_gate_up_sibling.1), channel_id=1, source_target_pairs={{0,4},{1,5},{2,6},{3,7},{4,0},{5,1},{6,2},{7,3},{8,12},{9,13},{10,... | collective-permute-start | bytes 17301512 | tf_op jit(solution)/shard_map/ppermute | solution.py:76
  236.4 44.7 %collective-permute-start.23 = (bf16[4,256,1536]{2,1,0:T(8,128)(2,1)}, bf16[4,256,1536]{2,1,0:T(8,128)(2,1)S(1)}, u32[]{:S(2)}, u32[]{:S(2)}) collective-permute-start(bf16[4,256,1536]{2,1,0:T(8,128)(2,1)} %grad_qkv_sibling.1), channel_id=1, source_target_pairs={{0,4},{1,5},{2,6},{3,7},{4,0},{5,1},{6,2},{7,3},{8,12},{9,13},{10,... | collective-permute-start | bytes 9437192 | tf_op jit(solution)/shard_map/ppermute | solution.py:76
  273.6 67.7 %collective-permute-start.30 = (bf16[4,256,512]{2,1,0:T(8,128)(2,1)}, bf16[4,256,512]{2,1,0:T(8,128)(2,1)}, u32[]{:S(2)}, u32[]{:S(2)}) collective-permute-start(bf16[4,256,512]{2,1,0:T(8,128)(2,1)} %grad_out_sibling.1), channel_id=1, source_target_pairs={{0,4},{1,5},{2,6},{3,7},{4,0},{5,1},{6,2},{7,3},{8,12},{9,13},{10,... | collective-permute-start | bytes 3145736 | tf_op jit(solution)/shard_map/ppermute | solution.py:76
  280.7 67.1 %collective-permute-start.45 = (bf16[2,704,512]{2,1,0:T(8,128)(2,1)}, bf16[2,704,512]{2,1,0:T(8,128)(2,1)S(1)}, u32[]{:S(2)}, u32[]{:S(2)}) collective-permute-start(bf16[2,704,512]{2,1,0:T(8,128)(2,1)} %get-tuple-element.87), channel_id=1, source_target_pairs={{0,1},{1,0},{2,3},{3,2},{4,6},{5,7},{6,4},{7,5},{8,9},{9,8},{10,11... | collective-permute-start | bytes 4325384 | tf_op jit(solution)/shard_map/ppermute | solution.py:76
  289.6 63.3 %collective-permute-start.24 = (bf16[2,256,1536]{2,1,0:T(8,128)(2,1)}, bf16[2,256,1536]{2,1,0:T(8,128)(2,1)S(1)}, u32[]{:S(2)}, u32[]{:S(2)}) collective-permute-start(bf16[2,256,1536]{2,1,0:T(8,128)(2,1)} %get-tuple-element.75), channel_id=1, source_target_pairs={{0,1},{1,0},{2,3},{3,2},{4,6},{5,7},{6,4},{7,5},{8,9},{9,8},{10,11... | collective-permute-start | bytes 4718600 | tf_op jit(solution)/shard_map/ppermute | solution.py:76
  295.9 62.2 %collective-permute-start.39 = (bf16[1,256,2816]{2,1,0:T(8,128)(2,1)}, bf16[1,256,2816]{2,1,0:T(8,128)(2,1)}, u32[]{:S(2)}, u32[]{:S(2)}) collective-permute-start(bf16[1,256,2816]{2,1,0:T(8,128)(2,1)} %slice.93), channel_id=1, source_target_pairs={{0,2},{1,3},{2,0},{3,1},{4,5},{5,4},{6,7},{7,6},{8,10},{9,11},{10,... | collective-permute-start | bytes 4325384 | tf_op jit(solution)/shard_map/ppermute | solution.py:76
  296.7 38.8 %collective-permute-start.19 = (f32[8,1024]{1,0:T(8,128)S(1)}, f32[8,1024]{1,0:T(8,128)S(1)}, u32[]{:S(2)}, u32[]{:S(2)}) collective-permute-start(f32[8,1024]{1,0:T(8,128)S(1)} %fusion.18), channel_id=1, source_target_pairs={{0,1},{1,0},{2,3},{3,2},{4,6},{5,7},{6,4},{7,5},{8,9},{9,8},{10,11... | collective-permute-start | bytes 98312 | tf_op jit(solution)/shard_map/ppermute | solution.py:76
  352.2 48.0 %collective-permute-start.46 = (bf16[1,704,512]{2,1,0:T(8,128)(2,1)}, bf16[1,704,512]{2,1,0:T(8,128)(2,1)}, u32[]{:S(2)}, u32[]{:S(2)}) collective-permute-start(bf16[1,704,512]{2,1,0:T(8,128)(2,1)} %slice.95), channel_id=1, source_target_pairs={{0,2},{1,3},{2,0},{3,1},{4,5},{5,4},{6,7},{7,6},{8,10},{9,11},{10,... | collective-permute-start | bytes 2162696 | tf_op jit(solution)/shard_map/ppermute | solution.py:76
  356.9 46.0 %collective-permute-start.25 = (bf16[1,256,1536]{2,1,0:T(8,128)(2,1)}, bf16[1,256,1536]{2,1,0:T(8,128)(2,1)}, u32[]{:S(2)}, u32[]{:S(2)}) collective-permute-start(bf16[1,256,1536]{2,1,0:T(8,128)(2,1)} %slice.82), channel_id=1, source_target_pairs={{0,2},{1,3},{2,0},{3,1},{4,5},{5,4},{6,7},{7,6},{8,10},{9,11},{10,... | collective-permute-start | bytes 2359304 | tf_op jit(solution)/shard_map/ppermute | solution.py:76
  360.9 44.6 %collective-permute-start.40 = (bf16[256,2816]{1,0:T(8,128)(2,1)}, bf16[256,2816]{1,0:T(8,128)(2,1)}, u32[]{:S(2)}, u32[]{:S(2)}) collective-permute-start(bf16[256,2816]{1,0:T(8,128)(2,1)} %fusion.1), channel_id=1, source_target_pairs={{0,8},{1,9},{2,10},{3,11},{4,12},{5,13},{6,14},{7,15},{24,16},{25,... | collective-permute-start | bytes 4325384 | tf_op jit(solution)/shard_map/ppermute | solution.py:76
  434.6 48.3 %collective-permute-start.49 = (bf16[704,512]{1,0:T(8,128)(2,1)S(1)}, bf16[704,512]{1,0:T(8,128)(2,1)S(1)}, u32[]{:S(2)}, u32[]{:S(2)}) collective-permute-start(bf16[704,512]{1,0:T(8,128)(2,1)S(1)} %add_convert_fusion.9), channel_id=1, source_target_pairs={{8,0},{9,1},{10,2},{11,3},{12,4},{13,5},{14,6},{15,7},{16,24},{17,... | collective-permute-start | bytes 2162696 | tf_op jit(solution)/shard_map/ppermute | solution.py:76
  436.3 88.0 %collective-permute-start.42 = (bf16[256,2816]{1,0:T(8,128)(2,1)S(1)}, bf16[256,2816]{1,0:T(8,128)(2,1)S(1)}, u32[]{:S(2)}, u32[]{:S(2)}) collective-permute-start(bf16[256,2816]{1,0:T(8,128)(2,1)S(1)} %add_convert_fusion.3), channel_id=1, source_target_pairs={{8,0},{9,1},{10,2},{11,3},{12,4},{13,5},{14,6},{15,7},{16,24},{17,... | collective-permute-start | bytes 4325384 | tf_op jit(solution)/shard_map/ppermute | solution.py:76
  437.8 80.8 %collective-permute-start.28 = (bf16[256,1536]{1,0:T(8,128)(2,1)S(1)}, bf16[256,1536]{1,0:T(8,128)(2,1)S(1)}, u32[]{:S(2)}, u32[]{:S(2)}) collective-permute-start(bf16[256,1536]{1,0:T(8,128)(2,1)S(1)} %add_convert_fusion.6), channel_id=1, source_target_pairs={{8,0},{9,1},{10,2},{11,3},{12,4},{13,5},{14,6},{15,7},{16,24},{17,... | collective-permute-start | bytes 2359304 | tf_op jit(solution)/shard_map/ppermute | solution.py:76
  (71 other events, 1059.7 us)

commit v2 on v1

v2 whole, which is shorter than its diff:
```python
import functools
import math

import jax
import jax.numpy as jnp
import numpy as np
from jax import lax
from jax.experimental import pallas as pl
from jax.experimental.pallas import tpu as pltpu
from jax.sharding import PartitionSpec as P

HEAD_DIM = 64
PAIR = 2 * HEAD_DIM
TILE = 256
GAIN_ROWS = 16
norm_eps = 1e-06
F32 = jnp.float32
BF16 = jnp.bfloat16
AXES = ("dp", "fsdp")
ANY = pl.BlockSpec(memory_space=pl.ANY)


def dot_nn(a, b):
    return lax.dot_general(a, b, (((1,), (0,)), ((), ())), preferred_element_type=F32)


def dot_nt(a, b):
    return lax.dot_general(a, b, (((1,), (1,)), ((), ())), preferred_element_type=F32)


def dot_tn(a, b):
    return lax.dot_general(a, b, (((0,), (0,)), ((), ())), preferred_element_type=F32)


def rotary_tables(count):
    half = HEAD_DIM // 2
    frequency = np.exp(
        -(np.arange(half, dtype=np.float32) * np.float32(2.0) / np.float32(HEAD_DIM))
        * np.float32(math.log(10000.0))
    ).astype(np.float32)
    angles = np.arange(count, dtype=np.float32)[:, None] * frequency[None, :]
    cosine = np.cos(angles.astype(np.float64)).astype(np.float32)
    sine = np.sin(angles.astype(np.float64)).astype(np.float32)
    cosine = np.concatenate([cosine] * 4, axis=1)
    sine = np.concatenate([-sine, sine, -sine, sine], axis=1)
    return cosine, sine


def swap_halves(x):
    half = HEAD_DIM // 2
    lane = lax.broadcasted_iota(jnp.int32, x.shape, 1)
    up = pltpu.roll(x, PAIR - half, 1)
    down = pltpu.roll(x, half, 1)
    return jnp.where((lane % HEAD_DIM) < half, up, down)


def bit_reverse(value, bits):
    out = 0
    for i in range(bits):
        out = out + ((value >> i) & 1) * (1 << (bits - 1 - i))
    return out


class Layout:
    def __init__(self, dp, fs):
        self.dp, self.fs = dp, fs
        self.bits = fs.bit_length() - 1
        self.line = dp // 2

    def perm(self, move):
        pairs = []
        for d in range(self.dp):
            for f in range(self.fs):
                target = move(d, f)
                if target is not None:
                    pairs.append((d * self.fs + f, target[0] * self.fs + target[1]))
        return pairs

    def send(self, x, move):
        return lax.ppermute(x, AXES, self.perm(move))

    def core(self, x):
        return self.send(x, lambda d, f: (d ^ 1, f))

    def step(self, x, i):
        bits = self.bits
        return self.send(x, lambda d, f: (d, f ^ (1 << (i if d % 2 == 0 else bits - 1 - i))))

    def index(self, length):
        d, f = lax.axis_index("dp"), lax.axis_index("fsdp")
        c = d % 2
        masks = jnp.arange(self.fs, dtype=jnp.int32)
        turned = bit_reverse(masks, self.bits)
        straight = c == 0
        mine = f ^ jnp.where(straight, masks, turned)
        other = f ^ jnp.where(straight, turned, masks)
        order = f ^ jnp.where(straight, turned, masks)
        head = jnp.stack([c, 1 - c, length, f]).astype(jnp.int32)
        return jnp.concatenate([head, mine, other, order]).astype(jnp.int32)

    def gather(self, half):
        pieces = [half]
        for i in range(self.bits):
            pieces = pieces + [self.step(piece, i) for piece in pieces]
        return pieces, [self.core(piece) for piece in pieces[1:]]

    def line_sum(self, total):
        size = self.line
        if size == 1:
            return total
        half = size // 2
        r = lax.axis_index("dp") // 2

        def hop(x, table):
            return self.send(
                x, lambda d, f: (table[d // 2] * 2 + d % 2, f) if d // 2 in table else None
            )

        for i in range(half - 1):
            got = hop(total, {i: i + 1, size - 1 - i: size - 2 - i})
            total = add_low(total, got)
        got = hop(total, {half - 1: half, half: half - 1})
        total = add_low(total, got)
        for i in range(half - 1):
            low, high = half - 1 - i, half + i
            got = hop(total, {low: low - 1, high: high + 1})
            total = jnp.where((r == low - 1) | (r == high + 1), got, total)
        return total

    def reduce(self, keep, send):
        for i in range(self.bits):
            got = self.step(send, i)
            total = add_low(keep, got)
            blocks = total.shape[0]
            if blocks > 1:
                keep, send = total[: blocks // 2], total[blocks // 2 :]
        return self.line_sum(total[0])

    def small_sum(self, x):
        x = x + self.core(x)
        for i in range(self.bits):
            x = x + self.step(x, i)
        reach = 1
        while reach < self.line:
            x = x + self.send(x, lambda d, f: ((((d // 2) ^ reach) * 2 + d % 2), f))
            reach *= 2
        return x


def add_low(a, b):
    return (a.astype(F32) + b.astype(F32)).astype(BF16)


IDX_HEAD = 4


def start(copies):
    for copy in copies:
        copy.start()


def wait(copies):
    for copy in copies:
        copy.wait()


def call(body, grid, in_specs, out_specs, out_shape, scratch, name, flops, nbytes, limit=56):
    return pl.pallas_call(
        body,
        grid_spec=pltpu.PrefetchScalarGridSpec(
            num_scalar_prefetch=1,
            grid=grid,
            in_specs=in_specs,
            out_specs=out_specs,
            scratch_shapes=scratch,
        ),
        out_shape=out_shape,
        compiler_params=pltpu.CompilerParams(vmem_limit_bytes=limit * 2**20),
        cost_estimate=pl.CostEstimate(
            flops=int(flops), bytes_accessed=int(nbytes), transcendentals=0
        ),
        name=name,
    )


def whole(shape):
    zeros = (0,) * len(shape)
    return pl.BlockSpec(shape, lambda *_: zeros)


def struct(shape, dtype):
    return jax.ShapeDtypeStruct(shape, dtype)


class Place:
    def __init__(self, lay):
        self.bits, self.count = lay.bits, lay.fs
        self.d, self.f = lax.axis_index("dp"), lax.axis_index("fsdp")
        self.c = lax.rem(self.d, 2)
        self.flips = []
        for i in range(self.bits):
            ahead, back = 1 << i, 1 << (self.bits - 1 - i)
            one = ahead * (1 - 2 * lax.rem(self.f // ahead, 2))
            two = back * (1 - 2 * lax.rem(self.f // back, 2))
            self.flips.append(one + self.c * (two - one))

    def shard(self, m):
        return self.f + sum(self.flips[i] for i in range(self.bits) if (m >> i) & 1)

    def partner(self, i):
        return (self.d, self.f + self.flips[i])

    def sibling(self):
        return (self.d + 1 - 2 * self.c, self.f)

    def group(self):
        others = []
        for m in range(1, self.count):
            others.append((self.d, self.shard(m)))
        return others


def remote(src, dst, send, recv, device):
    return pltpu.make_async_remote_copy(
        src_ref=src,
        dst_ref=dst,
        send_sem=send,
        recv_sem=recv,
        device_id=device,
        device_id_type=pl.DeviceIdType.MESH,
    )


class Gather:
    def __init__(self, place, own, full, sems, slot):
        self.place = place
        send, recv, cross_send, cross_recv, local = sems
        count = place.count
        rows, side = own.shape[0], own.shape[1] // 2
        column = pl.multiple_of(place.c * side, 128)
        self.link, self.cross = [None], [None]
        self.local = pltpu.make_async_copy(
            own, full.at[pl.ds(pl.multiple_of(place.f * rows, rows), rows), :], local.at[slot]
        )
        for m in range(1, count):
            step = m.bit_length() - 1
            before = m - (1 << step)

            def spot(piece):
                at = pl.multiple_of(place.shard(piece) * rows, rows)
                return full.at[pl.ds(at, rows), pl.ds(column, side)]

            source = own.at[:, pl.ds(column, side)] if before == 0 else spot(before)
            self.link.append(
                remote(
                    source,
                    spot(before),
                    send.at[slot * count + m],
                    recv.at[slot * count + m],
                    place.partner(step),
                )
            )
            self.cross.append(
                remote(
                    spot(m),
                    spot(m),
                    cross_send.at[slot * count + m],
                    cross_recv.at[slot * count + m],
                    place.sibling(),
                )
            )

    def begin(self):
        for i in range(self.place.bits):
            self.link[1 << i].start()

    def arrived(self, m):
        self.link[m].wait_recv()
        for i in range(m.bit_length(), self.place.bits):
            self.link[m + (1 << i)].start()
        self.cross[m].start()

    def complete(self):
        for copy in self.cross[1:]:
            copy.wait_recv()

    def drain(self):
        for copy in self.link[1:] + self.cross[1:]:
            copy.wait_send()


def forward_body(
    lay,
    lengths,
    tokens,
    first,
    cosine,
    sine,
    gain_in,
    cotangent,
    in_qkv,
    in_out,
    in_gate,
    in_up,
    in_down,
    full_qkv,
    full_out,
    full_gate,
    full_up,
    full_down,
    out_q,
    out_k,
    out_v,
    logs,
    hidden_one2,
    attended2,
    hidden_two2,
    out_after,
    out_gate,
    out_up,
    out_product,
    grad_down,
    gains,
    sums,
    w_qkv,
    w_out,
    w_gate,
    w_up,
    gain,
    hidden,
    queries,
    keys,
    values,
    attended,
    after,
    gate_pre,
    low_gate,
    low_up,
    product2,
    cot2,
    grad_low,
    turned,
    send,
    recv,
    cross_send,
    cross_recv,
    local,
    gain_send,
    gain_recv,
    swap_send,
    swap_recv,
    write,
):
    place = Place(lay)
    count, c = place.count, place.c
    rows, width = tokens.shape
    shard_rows = in_qkv.shape[0]
    ff = in_gate.shape[1]
    sibling = place.sibling()

    barrier = pltpu.get_barrier_semaphore()
    for device in [sibling] + place.group():
        pl.semaphore_signal(barrier, inc=1, device_id=device, device_id_type=pl.DeviceIdType.MESH)
    pl.semaphore_wait(barrier, count)

    sems = (send, recv, cross_send, cross_recv, local)
    g_qkv = Gather(place, in_qkv, w_qkv, sems, 0)
    g_out = Gather(place, in_out, w_out, sems, 1)
    g_gate = Gather(place, in_gate, w_gate, sems, 2)
    g_up = Gather(place, in_up, w_up, sems, 3)
    g_down = Gather(place, in_down, full_down, sems, 4)
    gathers = [g_qkv, g_out, g_gate, g_up, g_down]
    g_qkv.begin()
    gain_at = pl.multiple_of(place.f * shard_rows, shard_rows)
    gain_copies = []
    for m, device in enumerate(place.group()):
        gain_copies.append(
            remote(
                gain_in,
                gain.at[:, pl.ds(gain_at, shard_rows)],
                gain_send.at[m],
                gain_recv.at[m],
                device,
            )
        )
    gain_own = pltpu.make_async_copy(
        gain_in, gain.at[:, pl.ds(gain_at, shard_rows)], local.at[5]
    )
    start(gain_copies + [gain_own])
    for gather in gathers:
        gather.local.start()
    g_out.begin()

    writes = []

    def put(source, target):
        copy = pltpu.make_async_copy(source, target, write.at[len(writes)])
        copy.start()
        writes.append(copy)

    swaps = []

    def swap(source, target):
        slot = len(swaps)
        copy = remote(source, target, swap_send.at[slot], swap_recv.at[slot], sibling)
        copy.start()
        swaps.append(copy)
        return copy

    def share(source, target):
        put(source, target.at[pl.ds(0, rows), :])
        return swap(source, target.at[pl.ds(rows, rows), :])

    half = width // 2
    theirs = pl.multiple_of((1 - c) * half, 128)
    ours = pl.multiple_of(c * half, 128)
    cot_swap = swap(cotangent.at[:, pl.ds(theirs, half)], cot2.at[pl.ds(rows, rows), :])
    cot_own = pltpu.make_async_copy(
        cotangent.at[:, pl.ds(ours, half)], cot2.at[pl.ds(0, rows), :], local.at[6]
    )
    cot_own.start()

    inputs = tokens[...].astype(F32)
    inverse = lax.rsqrt(jnp.mean(inputs * inputs, axis=-1, keepdims=True) + norm_eps)
    for copy in gain_copies:
        copy.wait_recv()
    gain_own.wait()
    gains[0:1, :] = gain[0:1, :].astype(F32)
    gains[1:2, :] = gain[1:2, :].astype(F32)
    gains[2:8, :] = jnp.zeros((6, width), F32)
    hidden[...] = (inputs * inverse * gains[0:1, :]).astype(BF16)
    share(hidden, hidden_one2)
    for m in range(1, count):
        g_qkv.arrived(m)
        if m == count // 2:
            g_gate.begin()
    for m in range(1, count):
        g_out.arrived(m)
    g_qkv.local.wait()
    g_qkv.complete()
    put(w_qkv, full_qkv)
    g_up.begin()
    g_out.local.wait()
    g_out.complete()
    put(w_out, full_out)

    block = min(TILE, rows)

    @pl.loop(0, rows // block)
    def _(i):
        at = pl.ds(pl.multiple_of(i * block, block), block)
        cos, sin = cosine[at, :], sine[at, :]
        for which, out, scale in ((0, queries, HEAD_DIM**-0.5), (1, keys, 1.0)):
            raw = dot_nn(hidden[at, :], w_qkv[:, which * width : (which + 1) * width])
            for p in range(width // PAIR):
                x = raw[:, p * PAIR : (p + 1) * PAIR]
                low = (x * cos + swap_halves(x) * sin).astype(BF16)
                out[at, p * PAIR : (p + 1) * PAIR] = low * jnp.asarray(scale, BF16)

    sums[...] = jnp.zeros(sums.shape, F32)

    @pl.loop(0, rows // block)
    def _(i):
        at = pl.ds(pl.multiple_of(i * block, block), block)
        raw = dot_nn(hidden[at, :], w_qkv[:, 2 * width : 3 * width])
        kept = first[at, :].astype(F32)
        mixed = 0.5 * raw + 0.5 * kept
        values[at, :] = mixed.astype(BF16)
        sums[0:1, :] += jnp.sum(kept * kept, axis=0, keepdims=True)
        sums[1:2, :] += jnp.sum(mixed * mixed, axis=0, keepdims=True)

    put(queries, out_q)
    put(keys, out_k)
    put(values, out_v)
    length = lengths[0]

    def attend(begin, end):
        @pl.loop(begin, end)
        def _(p):
            at = pl.ds(pl.multiple_of(p * PAIR, PAIR), PAIR)
            q, k = queries[:, at], keys[:, at]
            v_t = values[:, at].T
            lane = lax.broadcasted_iota(jnp.int32, (rows, PAIR), 1)
            for head in range(2):
                inside = (lane // HEAD_DIM) == head
                k_head = jnp.where(inside, k, jnp.zeros_like(k))
                v_head = v_t[head * HEAD_DIM : (head + 1) * HEAD_DIM]
                for b in range(rows // block):
                    upto = (b + 1) * block
                    scores = dot_nt(k_head[:upto], q[b * block : upto])
                    key = lax.broadcasted_iota(jnp.int32, scores.shape, 0)
                    query = lax.broadcasted_iota(jnp.int32, (1, block), 1) + b * block
                    allowed = key <= jnp.minimum(query, length - 1)
                    scores = jnp.where(allowed, scores, -1e30)
                    peak = jnp.max(scores, axis=0, keepdims=True)
                    expo = jnp.exp(scores - peak)
                    total = jnp.sum(expo, axis=0, keepdims=True)
                    soft = (expo * (1.0 / total)).astype(BF16)
                    logs[p, head : head + 1, b * block : upto] = peak + jnp.log(total)
                    turned[head * HEAD_DIM : (head + 1) * HEAD_DIM, b * block : upto] = dot_nn(
                        v_head[:, :upto], soft
                    )
            attended[:, at] = turned[...].T.astype(BF16)

    pairs = width // PAIR
    logs[...] = jnp.zeros(logs.shape, F32)
    attend(0, pairs // 4)
    for m in range(1, count // 2):
        g_gate.arrived(m)
    attend(pairs // 4, pairs // 2)
    for m in range(count // 2, count):
        g_gate.arrived(m)
    g_down.begin()
    attend(pairs // 2, 3 * pairs // 4)
    for m in range(1, count // 2):
        g_up.arrived(m)
    attend(3 * pairs // 4, pairs)
    for m in range(count // 2, count):
        g_up.arrived(m)

    share(attended, attended2)

    @pl.loop(0, rows // block)
    def _(i):
        at = pl.ds(pl.multiple_of(i * block, block), block)
        x = tokens[at, :].astype(F32) + dot_nn(attended[at, :], w_out[...])
        after[at, :] = x
        scale = lax.rsqrt(jnp.mean(x * x, axis=-1, keepdims=True) + norm_eps)
        low_up[at, 0:width] = (x * scale * gains[1:2, :]).astype(BF16)

    put(after, out_after)
    hidden_two = low_up.at[:, pl.ds(0, width)]
    second = share(hidden_two, hidden_two2)
    second_put = writes[-1]
    g_gate.local.wait()
    g_gate.complete()
    put(w_gate, full_gate)

    @pl.loop(0, rows // block)
    def _(i):
        at = pl.ds(pl.multiple_of(i * block, block), block)
        gate_pre[at, :] = dot_nn(low_up[at, 0:width], w_gate[...])
        low_gate[at, :] = gate_pre[at, :].astype(BF16)

    put(low_gate, out_gate)
    g_up.local.wait()
    g_up.complete()
    put(w_up, full_up)
    for m in range(1, count // 2):
        g_down.arrived(m)
    second.wait_send()
    second_put.wait()

    @pl.loop(0, rows // block)
    def _(i):
        at = pl.ds(pl.multiple_of(i * block, block), block)
        up_proj = dot_nn(low_up[at, 0:width], w_up[...])
        gate_of = gate_pre[at, :]
        product2[at, :] = (gate_of * jax.nn.sigmoid(gate_of) * up_proj).astype(BF16)
        low_up[at, :] = up_proj.astype(BF16)

    put(low_up, out_up)
    own_product = product2.at[pl.ds(0, rows), :]
    put(own_product, out_product)
    product_swap = swap(own_product, product2.at[pl.ds(rows, rows), :])
    for m in range(count // 2, count):
        g_down.arrived(m)
    cot_own.wait()
    cot_swap.wait_recv()
    product_swap.wait_recv()

    @pl.loop(0, ff // TILE)
    def _(i):
        at = pl.ds(pl.multiple_of(i * TILE, TILE), TILE)
        grad_low[at, :] = dot_tn(product2[:, at], cot2[...]).astype(BF16)

    put(grad_low, grad_down)
    g_down.local.wait()
    g_down.complete()
    for gather in gathers:
        gather.drain()
    for copy in gain_copies:
        copy.wait_send()
    for copy in swaps:
        if copy is not cot_swap and copy is not product_swap:
            copy.wait_recv()
        if copy is not second:
            copy.wait_send()
    for copy in writes:
        if copy is not second_put:
            copy.wait()


def forward_kernel(lay, lengths, tokens, first, tables, gain_in, cotangent, w_qkv, w_out, w_gate, w_up, w_down):
    count = lay.fs
    rows, width = tokens.shape
    n, ff = w_qkv.shape[1], w_gate.shape[1]
    half = width // 2
    pairs = width // PAIR
    big = struct((rows, width), BF16)
    wide = struct((rows, ff), BF16)
    two = struct((2 * rows, width), BF16)
    dma = pltpu.SemaphoreType.DMA
    vmem = pl.BlockSpec(memory_space=pltpu.VMEM)
    weights = [(width, n), (width, width), (width, ff), (width, ff), (ff, width)]
    out_shape = (
        [struct(shape, BF16) for shape in weights]
        + [big, big, big, struct((pairs, 8, rows), F32)]
        + [two, two, two, struct((rows, width), F32), wide, wide, wide]
        + [struct((ff, half), BF16), struct((8, width), F32), struct((8, width), F32)]
    )
    out_specs = [ANY] * 8 + [vmem] + [ANY] * 8 + [vmem, vmem]
    return pl.pallas_call(
        functools.partial(forward_body, lay),
        in_specs=[pl.BlockSpec(memory_space=pltpu.SMEM)] + [vmem] * 4 + [vmem] + [ANY] * 6,
        out_specs=out_specs,
        out_shape=out_shape,
        scratch_shapes=[
            pltpu.VMEM((width, n), BF16),
            pltpu.VMEM((width, width), BF16),
            pltpu.VMEM((width, ff), BF16),
            pltpu.VMEM((width, ff), BF16),
            pltpu.VMEM((GAIN_ROWS, width), BF16),
            pltpu.VMEM((rows, width), BF16),
            pltpu.VMEM((rows, width), BF16),
            pltpu.VMEM((rows, width), BF16),
            pltpu.VMEM((rows, width), BF16),
            pltpu.VMEM((rows, width), BF16),
            pltpu.VMEM((rows, width), F32),
            pltpu.VMEM((rows, ff), F32),
            pltpu.VMEM((rows, ff), BF16),
            pltpu.VMEM((rows, ff), BF16),
            pltpu.VMEM((2 * rows, ff), BF16),
            pltpu.VMEM((2 * rows, half), BF16),
            pltpu.VMEM((ff, half), BF16),
            pltpu.VMEM((PAIR, rows), F32),
            dma((5 * count,)),
            dma((5 * count,)),
            dma((5 * count,)),
            dma((5 * count,)),
            dma((7,)),
            dma((count - 1,)),
            dma((count - 1,)),
            dma((5,)),
            dma((5,)),
            dma((16,)),
        ],
        compiler_params=pltpu.CompilerParams(
            collective_id=0, has_side_effects=True, vmem_limit_bytes=62 * 2**20
        ),
        cost_estimate=pl.CostEstimate(
            flops=2 * rows * width * (n + width + 3 * ff),
            bytes_accessed=60 * 2**20,
            transcendentals=0,
        ),
        name="forward",
    )(lengths, tokens, first, *tables, gain_in, cotangent, w_qkv, w_out, w_gate, w_up, w_down)


def attend_back_body(
    idx, queries, keys, values, grads, logs, cosine, sine, grad_q, grad_k, grad_v, grad_first, turned
):
    rows = queries.shape[0]
    block = min(TILE, rows)
    length = idx[2]
    lane = lax.broadcasted_iota(jnp.int32, (rows, PAIR), 1)
    q, k, v, g = queries[...], keys[...], values[...], grads[...]
    k_t = k.T
    sums_k, sums_v = [], []
    for head in range(2):
        inside = (lane // HEAD_DIM) == head
        k_head = jnp.where(inside, k, jnp.zeros_like(k))
        v_head = jnp.where(inside, v, jnp.zeros_like(v))
        k_turned = k_t[head * HEAD_DIM : (head + 1) * HEAD_DIM]
        parts_k, parts_v = [], []
        for b in range(rows // block):
            upto = (b + 1) * block
            q_block, g_block = q[b * block : upto], g[b * block : upto]
            scores = dot_nt(k_head[:upto], q_block)
            key = lax.broadcasted_iota(jnp.int32, scores.shape, 0)
            query = lax.broadcasted_iota(jnp.int32, (1, block), 1) + b * block
            log_total = logs[0, head : head + 1, b * block : upto]
            soft = jnp.where(
                key <= jnp.minimum(query, length - 1), jnp.exp(scores - log_total), 0.0
            )
            grad_soft = dot_nt(v_head[:upto], g_block)
            inner = jnp.sum(soft * grad_soft, axis=0, keepdims=True)
            grad_scores = (soft * (grad_soft - inner)).astype(BF16)
            turned[head * HEAD_DIM : (head + 1) * HEAD_DIM, b * block : upto] = dot_nn(
                k_turned[:, :upto], grad_scores
            )
            parts_k.append(dot_nn(grad_scores, q_block))
            parts_v.append(dot_nn(soft.astype(BF16), g_block))
        for parts, sums in ((parts_k, sums_k), (parts_v, sums_v)):
            rows_of = []
            for r in range(rows // block):
                piece = parts[r][r * block : (r + 1) * block]
                for later in parts[r + 1 :]:
                    piece = piece + later[r * block : (r + 1) * block]
                rows_of.append(piece)
            sums.append(jnp.concatenate(rows_of, axis=0))
    first_head = lane < HEAD_DIM
    cos, sin = cosine[...], sine[...]

    def back(x):
        return (x * cos - swap_halves(x) * sin).astype(BF16)

    grad_q[...] = back(turned[...].T * HEAD_DIM**-0.5)
    grad_k[...] = back(jnp.where(first_head, sums_k[0], sums_k[1]))
    half_v = 0.5 * jnp.where(first_head, sums_v[0], sums_v[1])
    grad_first[...] = half_v
    grad_v[...] = half_v.astype(BF16)


def attend_back_kernel(idx, queries, keys, values, grads, logs, tables):
    rows, width = queries.shape
    pairs = width // PAIR
    column = pl.BlockSpec((rows, PAIR), lambda p, _: (0, p))
    return call(
        attend_back_body,
        (pairs,),
        [column] * 4
        + [
            pl.BlockSpec((1, 8, rows), lambda p, _: (p, 0, 0)),
            whole(tables[0].shape),
            whole(tables[1].shape),
        ],
        [column] * 4,
        [struct((rows, width), BF16)] * 3 + [struct((rows, width), F32)],
        [pltpu.VMEM((PAIR, rows), F32)],
        "attend_back",
        20 * rows * rows * width,
        18 * rows * width,
        40,
    )(idx, queries, keys, values, grads, logs, *tables)


def down_body(idx, cotangent, after, gate, up, product, weight, grad_gate, grad_up, output, total):
    t = pl.program_id(0)

    @pl.when(t == 0)
    def _():
        total[...] = after[...]

    rows_of = weight[...]
    grad_product = dot_nt(cotangent[...], rows_of)
    gate_pre = gate[...].astype(F32)
    up_proj = up[...].astype(F32)
    sigma = jax.nn.sigmoid(gate_pre)
    grad_gate[...] = (
        grad_product * up_proj * sigma * (1.0 + gate_pre * (1.0 - sigma))
    ).astype(BF16)
    grad_up[...] = (grad_product * (gate_pre * sigma)).astype(BF16)
    total[...] += dot_nn(product[...], rows_of)

    @pl.when(t == pl.num_programs(0) - 1)
    def _():
        output[...] = total[...].astype(BF16)


def down_kernel(idx, cotangent, after, gate, up, product, weight):
    rows, width = cotangent.shape
    hidden = gate.shape[1]
    tile = pl.BlockSpec((rows, TILE), lambda t, _: (0, t))
    return call(
        down_body,
        (hidden // TILE,),
        [whole(cotangent.shape), whole(after.shape), tile, tile, tile]
        + [pl.BlockSpec((TILE, width), lambda t, _: (t, 0))],
        [tile, tile, whole((rows, width))],
        [
            struct((rows, hidden), BF16),
            struct((rows, hidden), BF16),
            struct((rows, width), BF16),
        ],
        [pltpu.VMEM((rows, width), F32)],
        "down",
        4 * rows * width * hidden,
        2 * width * hidden + 10 * rows * hidden,
    )(idx, cotangent, after, gate, up, product, weight)


def rms_back(grad, normed, inverse):
    return inverse * (grad - normed * jnp.mean(grad * normed, axis=-1, keepdims=True))


def mlp_back_body(idx, grad_gate, grad_up, after, cotangent, gains, w_out, w_gate, w_up, *rest):
    grad_after, grad_low, grad_attended, grad_gain, total = rest
    width = w_gate.shape[0]

    @pl.loop(0, width // TILE)
    def _(t):
        at = pl.multiple_of(t * TILE, TILE)
        total[:, pl.ds(at, TILE)] = dot_nt(grad_gate[...], w_gate[pl.ds(at, TILE), :]) + dot_nt(
            grad_up[...], w_up[pl.ds(at, TILE), :]
        )

    x = after[...]
    inverse = lax.rsqrt(jnp.mean(x * x, axis=-1, keepdims=True) + norm_eps)
    normed = x * inverse
    grad_hidden = total[...]
    grad_gain[...] = jnp.zeros(grad_gain.shape, F32)
    grad_gain[0:1, :] = jnp.sum(grad_hidden * normed, axis=0, keepdims=True)
    result = cotangent[...].astype(F32) + rms_back(grad_hidden * gains[1:2, :], normed, inverse)
    grad_after[...] = result
    grad_low[...] = result.astype(BF16)

    @pl.loop(0, width // TILE)
    def _(t):
        at = pl.multiple_of(t * TILE, TILE)
        grad_attended[:, pl.ds(at, TILE)] = dot_nt(
            grad_low[...], w_out[pl.ds(at, TILE), :]
        ).astype(BF16)


def mlp_back_kernel(idx, *operands):
    cotangent = operands[3]
    rows, width = cotangent.shape
    hidden = operands[0].shape[1]
    return call(
        mlp_back_body,
        (1,),
        [whole(item.shape) for item in operands],
        [whole((rows, width)), whole((rows, width)), whole((rows, width)), whole((8, width))],
        [
            struct((rows, width), F32),
            struct((rows, width), BF16),
            struct((rows, width), BF16),
            struct((8, width), F32),
        ],
        [pltpu.VMEM((rows, width), F32)],
        "mlp_back",
        2 * rows * width * (width + 2 * hidden),
        2 * width * (width + 2 * hidden) + 4 * rows * hidden + 12 * rows * width,
        62,
    )(idx, *operands)


def qkv_back_body(idx, grad_q, grad_k, grad_v, tokens, grad_after, gains, weight, grad_tokens, grad_gain, total):
    x = tokens[...].astype(F32)
    inverse = lax.rsqrt(jnp.mean(x * x, axis=-1, keepdims=True) + norm_eps)
    width = weight.shape[0]

    @pl.loop(0, width // TILE)
    def _(t):
        at = pl.multiple_of(t * TILE, TILE)
        block = pl.ds(at, TILE)
        total[:, block] = (
            dot_nt(grad_q[...], weight[block, 0:width])
            + dot_nt(grad_k[...], weight[block, width : 2 * width])
            + dot_nt(grad_v[...], weight[block, 2 * width : 3 * width])
        )

    normed = x * inverse
    grad_hidden = total[...]
    grad_gain[...] = jnp.zeros(grad_gain.shape, F32)
    grad_gain[0:1, :] = jnp.sum(grad_hidden * normed, axis=0, keepdims=True)
    grad_tokens[...] = grad_after[...] + rms_back(grad_hidden * gains[0:1, :], normed, inverse)


def qkv_back_kernel(idx, *operands):
    rows, width = operands[0].shape
    n = operands[-1].shape[1]
    return call(
        qkv_back_body,
        (1,),
        [whole(item.shape) for item in operands],
        [whole((rows, width)), whole((8, width))],
        [struct((rows, width), F32), struct((8, width), F32)],
        [pltpu.VMEM((rows, width), F32)],
        "qkv_back",
        2 * rows * width * n,
        2 * width * n + 16 * rows * width,
    )(idx, *operands)


def grad_sibling_body(parts, idx, turned, *rest):
    lefts, out = rest[:parts], rest[parts]
    side = lefts[0].shape[1]
    for i, left in enumerate(lefts):
        out[0, :, i * side : (i + 1) * side] = dot_tn(turned[...], left[...]).astype(BF16)


def grad_own_body(parts, blocks, idx, turned, *rest):
    lefts, got, keep, send = rest[:parts], rest[parts], rest[parts + 1], rest[parts + 2]
    side = lefts[0].shape[1]
    place = pl.program_id(0)

    def block(out):
        for i, left in enumerate(lefts):
            columns = slice(i * side, (i + 1) * side)
            summed = dot_tn(turned[...], left[...]) + got[0, :, columns].astype(F32)
            out[0, :, columns] = summed.astype(BF16)

    @pl.when(place < blocks // 2)
    def _():
        block(keep)

    @pl.when(place >= blocks // 2)
    def _():
        block(send)


def weight_grad(lay, idx, turned, lefts, name):
    blocks = lay.fs
    rows, total = lefts[0].shape[0], turned.shape[1]
    block = total // blocks
    half = [left.shape[1] // 2 for left in lefts]
    wide = sum(half)
    cost = (2 * rows * total * wide, 2 * rows * (total + wide) + 2 * total * wide)
    base = IDX_HEAD + 2 * blocks

    def shard(p, idx):
        return (0, idx[base + p])

    sibling = call(
        functools.partial(grad_sibling_body, len(lefts)),
        (blocks,),
        [pl.BlockSpec((rows, block), lambda p, idx: (0, p))]
        + [pl.BlockSpec((rows, side), lambda p, idx: (0, idx[1])) for side in half],
        [pl.BlockSpec((1, block, wide), lambda p, idx: (p, 0, 0))],
        [struct((blocks, block, wide), BF16)],
        [],
        name + "_sibling",
        *cost,
    )(idx, turned, *lefts)[0]
    got = lay.core(sibling)
    return call(
        functools.partial(grad_own_body, len(lefts), blocks),
        (blocks,),
        [pl.BlockSpec((rows, block), shard)]
        + [pl.BlockSpec((rows, side), lambda p, idx: (0, idx[0])) for side in half]
        + [pl.BlockSpec((1, block, wide), lambda p, idx: (idx[base + p], 0, 0))],
        [
            pl.BlockSpec((1, block, wide), lambda p, idx: (jnp.minimum(p, blocks // 2 - 1), 0, 0)),
            pl.BlockSpec((1, block, wide), lambda p, idx: (jnp.maximum(p - blocks // 2, 0), 0, 0)),
        ],
        [struct((blocks // 2, block, wide), BF16)] * 2,
        [],
        name + "_own",
        *cost,
    )(idx, turned, *lefts, got)


def finish_body(parts, idx, mine, other, *outs):
    low = idx[0] == 0
    at = 0
    for out in outs:
        side = out.shape[1] // 2
        a = mine[:, at : at + side].astype(F32)
        b = other[:, at : at + side].astype(F32)
        out[:, 0:side] = jnp.where(low, a, b)
        out[:, side:] = jnp.where(low, b, a)
        at += side


def finish(lay, idx, mine, widths, name):
    other = lay.core(mine)
    rows, wide = mine.shape
    block = rows // 4 if rows % 64 == 0 else rows
    return call(
        functools.partial(finish_body, len(widths)),
        (rows // block,),
        [pl.BlockSpec((block, wide), lambda p, _: (p, 0))] * 2,
        [pl.BlockSpec((block, 2 * side), lambda p, _: (p, 0)) for side in widths],
        [struct((rows, 2 * side), F32) for side in widths],
        [],
        name,
        0,
        12 * rows * wide,
    )(idx, mine, other)


def body(
    lay,
    tokens,
    first_values,
    lengths,
    gain_one,
    w_qkv,
    w_out,
    gain_two,
    w_gate,
    w_up,
    w_down,
    cotangent,
):
    rows, width = tokens.shape
    hidden = w_gate.shape[1]
    shard_rows = w_qkv.shape[0]
    idx = lay.index(lengths[0])
    tables = tuple(jnp.asarray(table) for table in rotary_tables(rows))
    c = lax.axis_index("dp") % 2
    gain_block = jnp.pad(jnp.stack([gain_one, gain_two]), ((0, GAIN_ROWS - 2), (0, 0)))
    (
        full_qkv,
        full_out,
        full_gate,
        full_up,
        full_down,
        queries,
        keys,
        values,
        logs,
        hidden_one,
        attended,
        hidden_two,
        after,
        gate,
        up,
        product,
        down_sum,
        gains,
        sums,
    ) = forward_kernel(
        lay, lengths, tokens, first_values, tables, gain_block, cotangent, w_qkv, w_out, w_gate, w_up, w_down
    )
    blocks = jnp.take(
        down_sum.reshape(lay.fs, -1, width // 2), idx[IDX_HEAD + 2 * lay.fs :], axis=0
    )
    total_down = lay.reduce(blocks[: lay.fs // 2], blocks[lay.fs // 2 :])
    grad_gate, grad_up, output = down_kernel(idx, cotangent, after, gate, up, product, full_down)
    keep, send = weight_grad(lay, idx, hidden_two, [grad_gate, grad_up], "grad_gate_up")
    total_gate_up = lay.reduce(keep, send)
    grad_after, grad_after_low, grad_attended, grad_gain_two = mlp_back_kernel(
        idx, grad_gate, grad_up, after, cotangent, gains, full_out, full_gate, full_up
    )
    keep, send = weight_grad(lay, idx, attended, [grad_after_low], "grad_out")
    total_out = lay.reduce(keep, send)
    grad_q, grad_k, grad_v, grad_first = attend_back_kernel(
        idx, queries, keys, values, grad_attended, logs, tables
    )
    keep, send = weight_grad(lay, idx, hidden_one, [grad_q, grad_k, grad_v], "grad_qkv")
    total_qkv = lay.reduce(keep, send)
    grad_tokens, grad_gain_one = qkv_back_kernel(
        idx, grad_q, grad_k, grad_v, tokens, grad_after, gains, full_qkv
    )

    small = jnp.concatenate(
        [
            grad_gain_one[0:1],
            grad_gain_two[0:1],
            jnp.pad(jnp.sum(sums, axis=1)[None], ((0, 5), (0, width - 8))),
        ]
    )
    small = lay.small_sum(small)
    at = lax.axis_index("fsdp") * shard_rows
    entry_count = rows * width * lay.dp * lay.fs
    shard_gain_one = lax.dynamic_slice(small[0], (at,), (shard_rows,))
    shard_gain_two = lax.dynamic_slice(small[1], (at,), (shard_rows,))
    first_norm = small[2, 0] / entry_count
    value_norm = small[2, 1] / entry_count

    (shard_down,) = finish(lay, idx, total_down, [width // 2], "finish_down")
    shard_gate, shard_up = finish(lay, idx, total_gate_up, [hidden // 2] * 2, "finish_gate_up")
    (shard_out,) = finish(lay, idx, total_out, [width // 2], "finish_out")
    third = width // 2
    other_qkv = lay.core(total_qkv)
    low = c == 0
    blocks = []
    for i in range(3):
        a = total_qkv[:, i * third : (i + 1) * third].astype(F32)
        b = other_qkv[:, i * third : (i + 1) * third].astype(F32)
        blocks += [jnp.where(low, a, b), jnp.where(low, b, a)]
    shard_qkv = jnp.concatenate(blocks, axis=1)
    return (
        output,
        grad_tokens,
        grad_first,
        shard_gain_one,
        shard_qkv,
        shard_out,
        shard_gain_two,
        shard_gate,
        shard_up,
        shard_down,
        first_norm,
        value_norm,
    )


def solution(mesh):
    both = P(AXES, None)
    rows = P("fsdp", None)
    in_specs = (both, both, P(AXES), P("fsdp"), rows, rows, P("fsdp"), rows, rows, rows, both)
    out_specs = (both, both, both, P("fsdp"), rows, rows, P("fsdp"), rows, rows, rows, P(), P())
    lay = Layout(mesh.shape["dp"], mesh.shape["fsdp"])
    return jax.shard_map(
        functools.partial(body, lay),
        mesh=mesh,
        in_specs=in_specs,
        out_specs=out_specs,
        check_vma=False,
    )
```

time: 540 us -> 472 us (0.87)
  waiting for transfers between devices: 240 us -> 121 us
  Pallas kernels: 187 us -> 255 us
  starting transfers between devices: 54 us -> 42.2 us
  local copies, waits for them, and re-layouts: 29.5 us -> 22.7 us
    ppermute x51 -> x32, waiting for transfers between devices: 240 us -> 121 us  [send(): return lax.ppermute(x, AXES, self.perm(move))]
    pallas_call x6 -> x4, Pallas kernels: 100 us -> 180 us  [the longest x1 131 us: forward_kernel(): pl.pallas_call(functools.partial(forward_body, lay), in_specs=[pl.BlockSp...]
    ppermute x51 -> x32, starting transfers between devices: 54 us -> 42.2 us  [send(): return lax.ppermute(x, AXES, self.perm(move))]
    pallas_call x4 -> x3, Pallas kernels: 28.3 us -> 21.9 us  [weight_grad(): call(functools.partial(grad_own_body, len(lefts), blocks), (blocks,), [pl...]
    unnamed x88 -> x46, local copies, waits for them, and re-layouts: 18.3 us -> 12.4 us
    pallas_call x4 -> x3, Pallas kernels: 24.9 us -> 18.9 us  [weight_grad(): call(functools.partial(grad_sibling_body, len(lefts)), (blocks,), [pl.Blo...]
  transfers between devices with their start and end apart: 51 -> 32, of which waited for: 13 -> 14; matrix products, arithmetic and copies ran while one was open for 5% -> 7% of each run, Pallas kernels for 29% -> 18%
where the time goes in v2:
time: 472 us; the launch traced here: 469 us
  Pallas kernels  255 us (54%)
  waiting for transfers between devices  121 us (26%)
  starting transfers between devices  42.2 us (9%)
  other arithmetic  23.9 us (5%)
  local copies, waits for them, and re-layouts  22.7 us (5%)
  between operations  5.38 us (1%)
    pallas_call x1, Pallas kernels, forward_kernel(): pl.pallas_call(functools.partial(forward_body, lay), in_specs=[pl.BlockSp...  131 us
    ppermute x32, waiting for transfers between devices, send(): return lax.ppermute(x, AXES, self.perm(move))  121 us
    ppermute x32, starting transfers between devices, send(): return lax.ppermute(x, AXES, self.perm(move))  42.2 us
    pallas_call x3, Pallas kernels, weight_grad(): call(functools.partial(grad_own_body, len(lefts), blocks), (blocks,), [pl...  21.9 us
    pallas_call x1, Pallas kernels, attend_back_kernel(): call(attend_back_body, (pairs,), [column] * 4 + [pl.BlockSpec((1, 8, rows...  20.4 us
    pallas_call x1, Pallas kernels, mlp_back_kernel(): call(mlp_back_body, (1,), [whole(item.shape) for item in operands], [whol...  19.5 us
    pallas_call x3, Pallas kernels, weight_grad(): call(functools.partial(grad_sibling_body, len(lefts)), (blocks,), [pl.Blo...  18.9 us
    pallas_call x1, Pallas kernels, down_kernel(): call(down_body, (hidden // TILE,), [whole(cotangent.shape), whole(after.s...  17.2 us
  transfers between devices with their start and end apart: 32, of which 14 were waited for; matrix products, arithmetic and copies ran while one was open for 7% of the time, Pallas kernels for 18%

profile of v2, /device:TPU:0, one launch (start us, length us, event | category | flops | bytes accessed | tf_op | source)
XLA Modules:
  0.0 469.4 jit_solution(13432013862826176280)
XLA Ops:
  3.9 131.1 %forward.1 = (bf16[1024,3072]{1,0:T(8,128)(2,1)}, bf16[1024,1024]{1,0:T(8,128)(2,1)}, bf16[1024,2816]{1,0:T(8,128)(2,1)}, bf16[1024,2816]{1,0:T(8,128)(2,1)}, bf...) custom-call(s32[1]{0:T(128)S(6)} %copy.30.lengths, ...), custom_call_target="tpu_custom_call" | custom-call | flops 13153337344 | bytes 62914560 | tf_op jit(solution)/shard_map/forward/pallas_call | solution.py:613
  135.0 17.2 %down.1 = (bf16[512,2816]{1,0:T(8,128)(2,1)}, bf16[512,2816]{1,0:T(8,128)(2,1)}, bf16[512,1024]{1,0:T(8,128)(2,1)}) custom-call(s32[16]{0:T(128)} %concatenate.9.idx, bf16[512,1024]{1,0:T(8,128)(2,1)} %cotangent.5, f32[512,1024]{1,0:T(8,128)} %get-tuple-element.52.after, bf16[512,2816]{1,0:T(8,128)(2,1)} %get-tuple-element.53.gate, ...), custom_call_target="tpu_custom_call" | custom-call | flops 5905580032 | bytes 20185088 | tf_op jit(solution)/shard_map/down/pallas_call | solution.py:765
  152.2 8.0 %grad_gate_up_sibling.1 = bf16[4,256,2816]{2,1,0:T(8,128)(2,1)} custom-call(s32[16]{0:T(128)} %concatenate.9.idx, bf16[1024,1024]{1,0:T(8,128)(2,1)} %get-tuple-element.86.turned, bf16[512,2816]{1,0:T(8,128)(2,1)} %get-tuple-element.61.grad_gate.rest_0_, bf16[512,2816]{1,0:T(8,128)(2,1)} %get-tuple-element.62.grad_up.rest_1_), custom_call_target="tpu_custom_call" | custom-call | flops 2952790016 | bytes 9699328 | tf_op jit(solution)/shard_map/grad_gate_up_sibling/pallas_call | solution.py:916
  160.2 9.6 %collective-permute-done.19.rest_2_ = bf16[4,256,2816]{2,1,0:T(8,128)(2,1)S(1)} collective-permute-done((bf16[4,256,2816]{2,1,0:T(8,128)(2,1)}, bf16[4,256,2816]{2,1,0:T(8,128)(2,1)S(1)}, u32[]{:S(2)}, u32[]{:S(2)}) %collective-permute-start.19) | collective-permute-done | bytes 5767200 | tf_op jit(solution)/shard_map/ppermute | solution.py:80
  172.3 9.8 %grad_gate_up_own.1 = (bf16[2,256,2816]{2,1,0:T(8,128)(2,1)}, bf16[2,256,2816]{2,1,0:T(8,128)(2,1)}) custom-call(s32[16]{0:T(128)} %concatenate.9.idx, bf16[1024,1024]{1,0:T(8,128)(2,1)} %get-tuple-element.86.turned, bf16[512,2816]{1,0:T(8,128)(2,1)} %get-tuple-element.61.grad_gate.rest_0_, bf16[512,2816]{1,0:T(8,128)(2,1)} %get-tuple-element.62.grad_up.rest_1_, ...), custom_call_target="tpu_custom_call" | custom-call | flops 2952790016 | bytes 9699328 | tf_op jit(solution)/shard_map/grad_gate_up_own/pallas_call | solution.py:928
  183.1 19.5 %mlp_back.1 = (f32[512,1024]{1,0:T(8,128)}, bf16[512,1024]{1,0:T(8,128)(2,1)}, bf16[512,1024]{1,0:T(8,128)(2,1)}, f32[8,1024]{1,0:T(8,128)}) custom-call(s32[16]{0:T(128)} %concatenate.9.idx, bf16[512,2816]{1,0:T(8,128)(2,1)} %get-tuple-element.61.grad_gate.rest_0_, bf16[512,2816]{1,0:T(8,128)(2,1)} %get-tuple-element.62.grad_up.rest_1_, ...), custom_call_target="tpu_custom_call" | custom-call | flops 6979321856 | bytes 25690112 | tf_op jit(solution)/shard_map/mlp_back/pallas_call | solution.py:820
  206.3 20.4 %attend_back.1 = (bf16[512,1024]{1,0:T(8,128)(2,1)S(1)}, bf16[512,1024]{1,0:T(8,128)(2,1)S(1)}, bf16[512,1024]{1,0:T(8,128)(2,1)S(1)}, f32[512,1024]{1,0:T(8,128)}) custom-call(s32[16]{0:T(128)S(1)} %copy-done.3, bf16[512,1024]{1,0:T(8,128)(2,1)S(1)} %copy-done.7, bf16[512,1024]{1,0:T(8,128)(2,1)S(1)} %copy-done.8, bf16[512,1024]{1,0:T(8,128)(2,1)S(1)} %copy-done.9, ...), custom_call_target="tpu_custom_call" | custom-call | flops 5368709120 | bytes 9437184 | tf_op jit(solution)/shard_map/attend_back/pallas_call | solution.py:719
  229.7 6.1 %grad_qkv_sibling.1 = bf16[4,256,1536]{2,1,0:T(8,128)(2,1)} custom-call(s32[16]{0:T(128)} %concatenate.9.idx, bf16[1024,1024]{1,0:T(8,128)(2,1)} %get-tuple-element.79.turned, bf16[512,1024]{1,0:T(8,128)(2,1)} %copy-done, bf16[512,1024]{1,0:T(8,128)(2,1)} %copy-done.1, bf16[512,1024]{1,0:T(8,128)(2,1)} %copy-done.2), custom_call_target="tpu_custom_call" | custom-call | flops 1610612736 | bytes 5767168 | tf_op jit(solution)/shard_map/grad_qkv_sibling/pallas_call | solution.py:916
  235.8 4.8 %grad_out_sibling.1 = bf16[4,256,512]{2,1,0:T(8,128)(2,1)} custom-call(s32[16]{0:T(128)} %concatenate.9.idx, bf16[1024,1024]{1,0:T(8,128)(2,1)} %get-tuple-element.82.turned, bf16[512,1024]{1,0:T(8,128)(2,1)} %get-tuple-element.83.rest_0_), custom_call_target="tpu_custom_call" | custom-call | flops 536870912 | bytes 2621440 | tf_op jit(solution)/shard_map/grad_out_sibling/pallas_call | solution.py:916
  245.2 5.1 %grad_out_own.1 = (bf16[2,256,512]{2,1,0:T(8,128)(2,1)}, bf16[2,256,512]{2,1,0:T(8,128)(2,1)}) custom-call(s32[16]{0:T(128)} %concatenate.9.idx, bf16[1024,1024]{1,0:T(8,128)(2,1)} %get-tuple-element.82.turned, bf16[512,1024]{1,0:T(8,128)(2,1)} %get-tuple-element.83.rest_0_, bf16[4,256,512]{2,1,0:T(8,128)(2,1)} %collective-permute-done.12.rest_1_), custom_call_target="tpu_custom_call" | custom-call | flops 536870912 | bytes 2621440 | tf_op jit(solution)/shard_map/grad_out_own/pallas_call | solution.py:928
  256.9 11.4 %collective-permute-done.26 = bf16[2,704,512]{2,1,0:T(8,128)(2,1)} collective-permute-done((bf16[2,704,512]{2,1,0:T(8,128)(2,1)S(1)}, bf16[2,704,512]{2,1,0:T(8,128)(2,1)}, u32[]{:S(2)}, u32[]{:S(2)}) %collective-permute-start.26) | collective-permute-done | bytes 1441824 | tf_op jit(solution)/shard_map/ppermute | solution.py:80
  272.1 7.3 %collective-permute-done.13 = bf16[2,256,512]{2,1,0:T(8,128)(2,1)S(1)} collective-permute-done((bf16[2,256,512]{2,1,0:T(8,128)(2,1)}, bf16[2,256,512]{2,1,0:T(8,128)(2,1)S(1)}, u32[]{:S(2)}, u32[]{:S(2)}) %collective-permute-start.13) | collective-permute-done | bytes 524320 | tf_op jit(solution)/shard_map/ppermute | solution.py:80
  281.3 7.0 %grad_qkv_own.1 = (bf16[2,256,1536]{2,1,0:T(8,128)(2,1)}, bf16[2,256,1536]{2,1,0:T(8,128)(2,1)}) custom-call(s32[16]{0:T(128)} %concatenate.9.idx, bf16[1024,1024]{1,0:T(8,128)(2,1)} %get-tuple-element.79.turned, bf16[512,1024]{1,0:T(8,128)(2,1)} %copy-done, bf16[512,1024]{1,0:T(8,128)(2,1)} %copy-done.1, bf16[512,1024]{1,0:T(8,128)(2,1)} %copy-done.2, ...), custom_call_target="tpu_custom_call" | custom-call | flops 1610612736 | bytes 5767168 | tf_op jit(solution)/shard_map/grad_qkv_own/pallas_call | solution.py:928
  289.3 12.0 %qkv_back.1 = (f32[512,1024]{1,0:T(8,128)}, f32[8,1024]{1,0:T(8,128)}) custom-call(s32[16]{0:T(128)} %concatenate.9.idx, bf16[512,1024]{1,0:T(8,128)(2,1)} %copy-done, bf16[512,1024]{1,0:T(8,128)(2,1)} %copy-done.1, bf16[512,1024]{1,0:T(8,128)(2,1)} %copy-done.2, bf16[512,1024]{1,0:T(8,128)(2,1)} %tokens.3, f32[512,1024]{1,0:T(8,128)} %get-tuple-element.72.grad_after, ...), custom_call_target="tpu_custom_call" | custom-call | flops 3221225472 | bytes 14680064 | tf_op jit(solution)/shard_map/qkv_back/pallas_call | solution.py:864
  320.3 9.4 %collective-permute-done.28 = bf16[704,512]{1,0:T(8,128)(2,1)S(1)} collective-permute-done((bf16[704,512]{1,0:T(8,128)(2,1)S(1)}, bf16[704,512]{1,0:T(8,128)(2,1)S(1)}, u32[]{:S(2)}, u32[]{:S(2)}) %collective-permute-start.28) | collective-permute-done | bytes 720928 | tf_op jit(solution)/shard_map/ppermute | solution.py:80
  331.7 6.4 %collective-permute-start.8 = (bf16[256,1536]{1,0:T(8,128)(2,1)S(1)}, bf16[256,1536]{1,0:T(8,128)(2,1)S(1)}, u32[]{:S(2)}, u32[]{:S(2)}) collective-permute-start(bf16[256,1536]{1,0:T(8,128)(2,1)S(1)} %fusion.1), channel_id=1, source_target_pairs={{0,8},{1,9},{2,10},{3,11},{4,12},{5,13},{6,14},{7,15},{24,16},{25,... | collective-permute-start | bytes 2359304 | tf_op jit(solution)/shard_map/ppermute | solution.py:80
  338.1 22.6 %collective-permute-done.22 = bf16[256,2816]{1,0:T(8,128)(2,1)S(1)} collective-permute-done((bf16[256,2816]{1,0:T(8,128)(2,1)S(1)}, bf16[256,2816]{1,0:T(8,128)(2,1)S(1)}, u32[]{:S(2)}, u32[]{:S(2)}) %collective-permute-start.22) | collective-permute-done | bytes 1441824 | tf_op jit(solution)/shard_map/ppermute | solution.py:80
  362.8 10.0 %collective-permute-done.8 = bf16[256,1536]{1,0:T(8,128)(2,1)S(1)} collective-permute-done((bf16[256,1536]{1,0:T(8,128)(2,1)S(1)}, bf16[256,1536]{1,0:T(8,128)(2,1)S(1)}, u32[]{:S(2)}, u32[]{:S(2)}) %collective-permute-start.8) | collective-permute-done | bytes 786464 | tf_op jit(solution)/shard_map/ppermute | solution.py:80
  378.5 4.4 collective-permute-start.3
  398.2 15.9 %collective-permute-done.30 = bf16[704,512]{1,0:T(8,128)(2,1)S(1)} collective-permute-done((bf16[704,512]{1,0:T(8,128)(2,1)S(1)}, bf16[704,512]{1,0:T(8,128)(2,1)S(1)}, u32[]{:S(2)}, u32[]{:S(2)}) %collective-permute-start.30) | collective-permute-done | bytes 720928 | tf_op jit(solution)/shard_map/ppermute | solution.py:80
  419.6 3.9 finish_out.1
  424.3 4.6 finish_down.1
  432.3 23.4 %collective-permute-done.24 = bf16[256,2816]{1,0:T(8,128)(2,1)} collective-permute-done((bf16[256,2816]{1,0:T(8,128)(2,1)S(1)}, bf16[256,2816]{1,0:T(8,128)(2,1)}, u32[]{:S(2)}, u32[]{:S(2)}) %collective-permute-start.24) | collective-permute-done | bytes 1441824 | tf_op jit(solution)/shard_map/ppermute | solution.py:80
  461.7 5.4 %finish_gate_up.1 = (f32[256,2816]{1,0:T(8,128)}, f32[256,2816]{1,0:T(8,128)}) custom-call(s32[16]{0:T(128)} %concatenate.9.idx, bf16[256,2816]{1,0:T(8,128)(2,1)} %copy-done.13, bf16[256,2816]{1,0:T(8,128)(2,1)} %copy-done.16), custom_call_target="tpu_custom_call" | custom-call | bytes 8650752 | tf_op jit(solution)/shard_map/finish_gate_up/pallas_call | solution.py:961
  (153 shorter events, 88.8 us)
Async XLA Ops:
  182.0 69.3 %collective-permute-start.20 = (bf16[2,256,2816]{2,1,0:T(8,128)(2,1)}, bf16[2,256,2816]{2,1,0:T(8,128)(2,1)}, u32[]{:S(2)}, u32[]{:S(2)}) collective-permute-start(bf16[2,256,2816]{2,1,0:T(8,128)(2,1)} %get-tuple-element.88), channel_id=1, source_target_pairs={{0,1},{1,0},{2,3},{3,2},{4,6},{5,7},{6,4},{7,5},{8,9},{9,8},{10,11... | collective-permute-start | bytes 8650760 | tf_op jit(solution)/shard_map/ppermute | solution.py:80
  235.8 45.5 %collective-permute-start.5 = (bf16[4,256,1536]{2,1,0:T(8,128)(2,1)}, bf16[4,256,1536]{2,1,0:T(8,128)(2,1)}, u32[]{:S(2)}, u32[]{:S(2)}) collective-permute-start(bf16[4,256,1536]{2,1,0:T(8,128)(2,1)} %grad_qkv_sibling.1), channel_id=1, source_target_pairs={{0,4},{1,5},{2,6},{3,7},{4,0},{5,1},{6,2},{7,3},{8,12},{9,13},{10,... | collective-permute-start | bytes 9437192 | tf_op jit(solution)/shard_map/ppermute | solution.py:80
  244.1 24.2 %collective-permute-start.26 = (bf16[2,704,512]{2,1,0:T(8,128)(2,1)S(1)}, bf16[2,704,512]{2,1,0:T(8,128)(2,1)}, u32[]{:S(2)}, u32[]{:S(2)}) collective-permute-start(bf16[2,704,512]{2,1,0:T(8,128)(2,1)S(1)} %slice.105), channel_id=1, source_target_pairs={{0,1},{1,0},{2,3},{3,2},{4,6},{5,7},{6,4},{7,5},{8,9},{9,8},{10,11... | collective-permute-start | bytes 4325384 | tf_op jit(solution)/shard_map/ppermute | solution.py:80
  250.3 29.1 %collective-permute-start.13 = (bf16[2,256,512]{2,1,0:T(8,128)(2,1)}, bf16[2,256,512]{2,1,0:T(8,128)(2,1)S(1)}, u32[]{:S(2)}, u32[]{:S(2)}) collective-permute-start(bf16[2,256,512]{2,1,0:T(8,128)(2,1)} %get-tuple-element.85), channel_id=1, source_target_pairs={{0,1},{1,0},{2,3},{3,2},{4,6},{5,7},{6,4},{7,5},{8,9},{9,8},{10,11... | collective-permute-start | bytes 1572872 | tf_op jit(solution)/shard_map/ppermute | solution.py:80
  255.9 54.5 %collective-permute-start.21 = (bf16[1,256,2816]{2,1,0:T(8,128)(2,1)}, bf16[1,256,2816]{2,1,0:T(8,128)(2,1)}, u32[]{:S(2)}, u32[]{:S(2)}) collective-permute-start(bf16[1,256,2816]{2,1,0:T(8,128)(2,1)} %slice.103), channel_id=1, source_target_pairs={{0,2},{1,3},{2,0},{3,1},{4,5},{5,4},{6,7},{7,6},{8,10},{9,11},{10,... | collective-permute-start | bytes 4325384 | tf_op jit(solution)/shard_map/ppermute | solution.py:80
  271.1 36.5 %collective-permute-start.27 = (bf16[1,704,512]{2,1,0:T(8,128)(2,1)}, bf16[1,704,512]{2,1,0:T(8,128)(2,1)}, u32[]{:S(2)}, u32[]{:S(2)}) collective-permute-start(bf16[1,704,512]{2,1,0:T(8,128)(2,1)} %slice.107), channel_id=1, source_target_pairs={{0,2},{1,3},{2,0},{3,1},{4,5},{5,4},{6,7},{7,6},{8,10},{9,11},{10,... | collective-permute-start | bytes 2162696 | tf_op jit(solution)/shard_map/ppermute | solution.py:80
  280.3 22.6 %collective-permute-start.14 = (bf16[1,256,512]{2,1,0:T(8,128)(2,1)}, bf16[1,256,512]{2,1,0:T(8,128)(2,1)}, u32[]{:S(2)}, u32[]{:S(2)}) collective-permute-start(bf16[1,256,512]{2,1,0:T(8,128)(2,1)} %slice.100), channel_id=1, source_target_pairs={{0,2},{1,3},{2,0},{3,1},{4,5},{5,4},{6,7},{7,6},{8,10},{9,11},{10,... | collective-permute-start | bytes 786440 | tf_op jit(solution)/shard_map/ppermute | solution.py:80
  288.3 25.3 %collective-permute-start.6 = (bf16[2,256,1536]{2,1,0:T(8,128)(2,1)}, bf16[2,256,1536]{2,1,0:T(8,128)(2,1)}, u32[]{:S(2)}, u32[]{:S(2)}) collective-permute-start(bf16[2,256,1536]{2,1,0:T(8,128)(2,1)} %get-tuple-element.81), channel_id=1, source_target_pairs={{0,1},{1,0},{2,3},{3,2},{4,6},{5,7},{6,4},{7,5},{8,9},{9,8},{10,11... | collective-permute-start | bytes 4718600 | tf_op jit(solution)/shard_map/ppermute | solution.py:80
  303.9 15.0 %collective-permute-start.15 = (bf16[256,512]{1,0:T(8,128)(2,1)S(1)}, bf16[256,512]{1,0:T(8,128)(2,1)S(1)}, u32[]{:S(2)}, u32[]{:S(2)}) collective-permute-start(bf16[256,512]{1,0:T(8,128)(2,1)S(1)} %fusion.9), channel_id=1, source_target_pairs={{0,8},{1,9},{2,10},{3,11},{4,12},{5,13},{6,14},{7,15},{24,16},{25,... | collective-permute-start | bytes 786440 | tf_op jit(solution)/shard_map/ppermute | solution.py:80
  309.1 20.6 %collective-permute-start.28 = (bf16[704,512]{1,0:T(8,128)(2,1)S(1)}, bf16[704,512]{1,0:T(8,128)(2,1)S(1)}, u32[]{:S(2)}, u32[]{:S(2)}) collective-permute-start(bf16[704,512]{1,0:T(8,128)(2,1)S(1)} %fusion.2), channel_id=1, source_target_pairs={{0,8},{1,9},{2,10},{3,11},{4,12},{5,13},{6,14},{7,15},{24,16},{25,... | collective-permute-start | bytes 2162696 | tf_op jit(solution)/shard_map/ppermute | solution.py:80
  312.1 48.5 %collective-permute-start.22 = (bf16[256,2816]{1,0:T(8,128)(2,1)S(1)}, bf16[256,2816]{1,0:T(8,128)(2,1)S(1)}, u32[]{:S(2)}, u32[]{:S(2)}) collective-permute-start(bf16[256,2816]{1,0:T(8,128)(2,1)S(1)} %fusion), channel_id=1, source_target_pairs={{0,8},{1,9},{2,10},{3,11},{4,12},{5,13},{6,14},{7,15},{24,16},{25,... | collective-permute-start | bytes 4325384 | tf_op jit(solution)/shard_map/ppermute | solution.py:80
  315.4 16.0 %collective-permute-start.7 = (bf16[1,256,1536]{2,1,0:T(8,128)(2,1)S(1)}, bf16[1,256,1536]{2,1,0:T(8,128)(2,1)S(1)}, u32[]{:S(2)}, u32[]{:S(2)}) collective-permute-start(bf16[1,256,1536]{2,1,0:T(8,128)(2,1)S(1)} %slice.92), channel_id=1, source_target_pairs={{0,2},{1,3},{2,0},{3,1},{4,5},{5,4},{6,7},{7,6},{8,10},{9,11},{10,... | collective-permute-start | bytes 2359304 | tf_op jit(solution)/shard_map/ppermute | solution.py:80
  317.8 56.7 %collective-permute-start.1 = (f32[8,1024]{1,0:T(8,128)S(1)}, f32[8,1024]{1,0:T(8,128)S(1)}, u32[]{:S(2)}, u32[]{:S(2)}) collective-permute-start(f32[8,1024]{1,0:T(8,128)S(1)} %fusion.24), channel_id=1, source_target_pairs={{0,1},{1,0},{2,3},{3,2},{4,6},{5,7},{6,4},{7,5},{8,9},{9,8},{10,11... | collective-permute-start | bytes 98312 | tf_op jit(solution)/shard_map/ppermute | solution.py:80
  319.0 67.8 %collective-permute-start.16 = (bf16[256,512]{1,0:T(8,128)(2,1)S(1)}, bf16[256,512]{1,0:T(8,128)(2,1)}, u32[]{:S(2)}, u32[]{:S(2)}) collective-permute-start(bf16[256,512]{1,0:T(8,128)(2,1)S(1)} %add_convert_fusion.14), channel_id=1, source_target_pairs={{8,16},{9,17},{10,18},{11,19},{12,20},{13,21},{14,22},{15,23},{16,... | collective-permute-start | bytes 786440 | tf_op jit(solution)/shard_map/ppermute | solution.py:80
  329.9 59.1 %collective-permute-start.29 = (bf16[704,512]{1,0:T(8,128)(2,1)S(1)}, bf16[704,512]{1,0:T(8,128)(2,1)}, u32[]{:S(2)}, u32[]{:S(2)}) collective-permute-start(bf16[704,512]{1,0:T(8,128)(2,1)S(1)} %add_convert_fusion.10), channel_id=1, source_target_pairs={{8,16},{9,17},{10,18},{11,19},{12,20},{13,21},{14,22},{15,23},{16,... | collective-permute-start | bytes 2162696 | tf_op jit(solution)/shard_map/ppermute | solution.py:80
  331.7 41.1 %collective-permute-start.8 = (bf16[256,1536]{1,0:T(8,128)(2,1)S(1)}, bf16[256,1536]{1,0:T(8,128)(2,1)S(1)}, u32[]{:S(2)}, u32[]{:S(2)}) collective-permute-start(bf16[256,1536]{1,0:T(8,128)(2,1)S(1)} %fusion.1), channel_id=1, source_target_pairs={{0,8},{1,9},{2,10},{3,11},{4,12},{5,13},{6,14},{7,15},{24,16},{25,... | collective-permute-start | bytes 2359304 | tf_op jit(solution)/shard_map/ppermute | solution.py:80
  361.0 34.2 %collective-permute-start.23 = (bf16[256,2816]{1,0:T(8,128)(2,1)S(1)}, bf16[256,2816]{1,0:T(8,128)(2,1)}, u32[]{:S(2)}, u32[]{:S(2)}) collective-permute-start(bf16[256,2816]{1,0:T(8,128)(2,1)S(1)} %add_convert_fusion.4), channel_id=1, source_target_pairs={{8,16},{9,17},{10,18},{11,19},{12,20},{13,21},{14,22},{15,23},{16,... | collective-permute-start | bytes 4325384 | tf_op jit(solution)/shard_map/ppermute | solution.py:80
  372.9 18.7 %collective-permute-start.9 = (bf16[256,1536]{1,0:T(8,128)(2,1)S(1)}, bf16[256,1536]{1,0:T(8,128)(2,1)}, u32[]{:S(2)}, u32[]{:S(2)}) collective-permute-start(bf16[256,1536]{1,0:T(8,128)(2,1)S(1)} %add_convert_fusion.7), channel_id=1, source_target_pairs={{8,16},{9,17},{10,18},{11,19},{12,20},{13,21},{14,22},{15,23},{16,... | collective-permute-start | bytes 2359304 | tf_op jit(solution)/shard_map/ppermute | solution.py:80
  384.8 29.4 %collective-permute-start.4 = (f32[8,1024]{1,0:T(8,128)S(1)}, f32[8,1024]{1,0:T(8,128)S(1)}, u32[]{:S(2)}, u32[]{:S(2)}) collective-permute-start(f32[8,1024]{1,0:T(8,128)S(1)} %add.113), channel_id=1, source_target_pairs={{0,16},{1,17},{2,18},{3,19},{4,20},{5,21},{6,22},{7,23},{8,24},{9,... | collective-permute-start | bytes 98312 | tf_op jit(solution)/shard_map/ppermute | solution.py:80
  387.8 28.5 %collective-permute-start.17 = (bf16[256,512]{1,0:T(8,128)(2,1)S(1)}, bf16[256,512]{1,0:T(8,128)(2,1)}, u32[]{:S(2)}, u32[]{:S(2)}) collective-permute-start(bf16[256,512]{1,0:T(8,128)(2,1)S(1)} %add_convert_fusion.13), channel_id=1, source_target_pairs={{8,0},{9,1},{10,2},{11,3},{12,4},{13,5},{14,6},{15,7},{16,24},{17,... | collective-permute-start | bytes 786440 | tf_op jit(solution)/shard_map/ppermute | solution.py:80
  390.4 23.7 %collective-permute-start.30 = (bf16[704,512]{1,0:T(8,128)(2,1)S(1)}, bf16[704,512]{1,0:T(8,128)(2,1)S(1)}, u32[]{:S(2)}, u32[]{:S(2)}) collective-permute-start(bf16[704,512]{1,0:T(8,128)(2,1)S(1)} %add_convert_fusion.9), channel_id=1, source_target_pairs={{8,0},{9,1},{10,2},{11,3},{12,4},{13,5},{14,6},{15,7},{16,24},{17,... | collective-permute-start | bytes 2162696 | tf_op jit(solution)/shard_map/ppermute | solution.py:80
  393.9 37.1 %collective-permute-start.10 = (bf16[256,1536]{1,0:T(8,128)(2,1)}, bf16[256,1536]{1,0:T(8,128)(2,1)}, u32[]{:S(2)}, u32[]{:S(2)}) collective-permute-start(bf16[256,1536]{1,0:T(8,128)(2,1)} %add_convert_fusion.6), channel_id=1, source_target_pairs={{8,0},{9,1},{10,2},{11,3},{12,4},{13,5},{14,6},{15,7},{16,24},{17,... | collective-permute-start | bytes 2359304 | tf_op jit(solution)/shard_map/ppermute | solution.py:80
  396.9 58.9 %collective-permute-start.24 = (bf16[256,2816]{1,0:T(8,128)(2,1)S(1)}, bf16[256,2816]{1,0:T(8,128)(2,1)}, u32[]{:S(2)}, u32[]{:S(2)}) collective-permute-start(bf16[256,2816]{1,0:T(8,128)(2,1)S(1)} %add_convert_fusion.3), channel_id=1, source_target_pairs={{8,0},{9,1},{10,2},{11,3},{12,4},{13,5},{14,6},{15,7},{16,24},{17,... | collective-permute-start | bytes 4325384 | tf_op jit(solution)/shard_map/ppermute | solution.py:80
  432.3 25.1 %collective-permute-start.11 = (bf16[256,1536]{1,0:T(8,128)(2,1)S(1)}, bf16[256,1536]{1,0:T(8,128)(2,1)S(1)}, u32[]{:S(2)}, u32[]{:S(2)}) collective-permute-start(bf16[256,1536]{1,0:T(8,128)(2,1)S(1)} %broadcast_select_fusion.2), channel_id=1, source_target_pairs={{0,4},{1,5},{2,6},{3,7},{4,0},{5,1},{6,2},{7,3},{8,12},{9,13},{10,... | collective-permute-start | bytes 2359304 | tf_op jit(solution)/shard_map/ppermute | solution.py:80
  (31 other events, 235.2 us)
